TPU v7x, 32 devices: a whole 2x2x4 slice. The times are simulated.
32 devices in a mesh: src: 8 (over z, x), rcv: 4 (over y, core).
Axes of the slice: x: 2, y: 2, z: 4, core: 2. Of those that a mesh axis runs over, the one named last changes fastest.
Arguments:
- raw_samples: bfloat16 [12, 4096, 1024], P('rcv', 'src'), may hold values from -400 to 400
- channel_of_row: int32 [4096], P('src'), may hold values from 0 to 4095, as said below
- live_channels: int32 [4096], P('src'), may hold values 0 or 1
- band_reach: int32 [4096], P('src'), may hold values from 1 to 2047
- bin_taper: float32 [64], replicated, may hold values from 0.5 to 2
Outputs:
- correlations: bfloat16 [4096, 65536], P('src', 'rcv')
Inputs may be any that keep to these rules, and one draw needn't show every extreme that they name: `channel_of_row`: rows 512 s to 512 (s + 1) - 1 hold, in some order, each channel c with c % 8 == s once.
All inputs are finite; a program needn't handle non-finite values. No bound on the sum of `live_channels` on one device may be relied on, other than what follows from the above.
Results may differ from a plain program's by a relative error of at most 0.0081.
Values may be sent and summed in bfloat16 or wider, within the bound.
A program may use at most 128 MiB of HBM per device.

v0:
```python
import math

import jax
import jax.numpy as jnp
from jax import lax
from jax.sharding import PartitionSpec as P

L = 1024
F = 64
K0 = 32
HW = 64
LAGS = 32


norm_floor = 1e-05
water_level = 0.3


def from_behind(block, axis, distance):
    devices = range(lax.axis_size(axis))
    route = [(i - distance, i) for i in devices if i - distance in devices]
    return lax.ppermute(block, axis, route)


def basis_table():
    sample_index = jnp.arange(L, dtype=jnp.int32)
    bin_index = jnp.arange(F, dtype=jnp.int32) + K0
    phase = jnp.mod(sample_index[:, None] * bin_index[None, :], L)
    angle = phase.astype(jnp.float32) * (2.0 * math.pi / L)
    return jnp.concatenate([jnp.cos(angle), -jnp.sin(angle)], axis=1).astype(jnp.bfloat16)


def lag_table():
    bin_index = jnp.arange(F, dtype=jnp.int32) + K0
    lag_index = jnp.arange(LAGS, dtype=jnp.int32) - LAGS // 2
    phase = jnp.mod(bin_index[:, None] * lag_index[None, :], L)
    angle = phase.astype(jnp.float32) * (2.0 * math.pi / L)
    table = jnp.concatenate([jnp.cos(angle), jnp.sin(angle)], axis=0) * (1.0 / math.sqrt(F))
    return table.astype(jnp.bfloat16)


def window_tables(block):
    source = jnp.arange(block, dtype=jnp.int32)[:, None]
    target = jnp.arange(block, dtype=jnp.int32)[None, :]
    middle = (jnp.abs(source - target) <= HW).astype(jnp.bfloat16)
    before = (block + target - source <= HW).astype(jnp.bfloat16)
    after = (block + source - target <= HW).astype(jnp.bfloat16)
    return (middle, before, after)


def whiten_rows(samples, bin_taper):
    row_count = samples.shape[0]
    block = min(128, L)
    block_count = L // block
    magnitude = jnp.abs(samples).reshape(row_count, block_count, block)
    zero_block = jnp.zeros((row_count, 1, block), jnp.bfloat16)
    earlier = jnp.concatenate([zero_block, magnitude[:, :-1]], axis=1)
    later = jnp.concatenate([magnitude[:, 1:], zero_block], axis=1)
    middle, before, after = window_tables(block)
    window_sum = jnp.einsum("rnu,uv->rnv", magnitude, middle, preferred_element_type=jnp.float32)
    window_sum = window_sum + jnp.einsum(
        "rnu,uv->rnv", earlier, before, preferred_element_type=jnp.float32
    )
    window_sum = window_sum + jnp.einsum(
        "rnu,uv->rnv", later, after, preferred_element_type=jnp.float32
    )
    window_sum = window_sum.reshape(row_count, L)
    positions = jnp.arange(L, dtype=jnp.int32)
    upper = jnp.minimum(positions + HW, L - 1)
    lower = jnp.maximum(positions - HW, 0)
    counts = (upper - lower + 1).astype(jnp.float32)
    normed = (samples.astype(jnp.float32) / (window_sum / counts + norm_floor)).astype(jnp.bfloat16)
    spectrum = jnp.dot(normed, basis_table(), preferred_element_type=jnp.float32)
    real_part = spectrum[:, :F]
    imag_part = spectrum[:, F:]
    amplitude = jnp.sqrt(real_part * real_part + imag_part * imag_part)
    padded = jnp.pad(amplitude, ((0, 0), (1, 1)))
    neighbours = padded[:, :-2] + padded[:, 1:-1] + padded[:, 2:]
    bins = jnp.arange(F, dtype=jnp.int32)
    bin_counts = jnp.where((bins == 0) | (bins == F - 1), 2.0, 3.0).astype(jnp.float32)
    smooth = neighbours / bin_counts
    level = jnp.maximum(
        smooth, water_level * (jnp.mean(amplitude, axis=1, keepdims=True) + norm_floor)
    )
    factor = bin_taper[None, :] / level
    return jnp.concatenate([real_part * factor, imag_part * factor], axis=1).astype(jnp.bfloat16)


def body(raw_samples, channel_of_row, live_channels, band_reach, bin_taper):
    src_count = lax.axis_size("src")
    rcv_count = lax.axis_size("rcv")
    src_place = lax.axis_index("src")
    rcv_place = lax.axis_index("rcv")
    win_local, block_rows, sample_count = raw_samples.shape
    white = whiten_rows(raw_samples.reshape(win_local * block_rows, sample_count), bin_taper)
    white = white.reshape(win_local, block_rows, 2 * F)
    ordering = jnp.argsort(channel_of_row // src_count)
    ordered = jnp.take(white, ordering, axis=1)
    per_target = block_rows // src_count
    grouped = ordered.reshape(win_local, src_count, per_target, 1, 2 * F)
    arrived = lax.all_to_all(grouped, "src", split_axis=1, concat_axis=3, tiled=True)
    own_block = (
        arrived.reshape(win_local, block_rows, 2 * F)
        * live_channels.astype(jnp.bfloat16)[None, :, None]
    )
    sources = lax.all_gather(own_block, "rcv", axis=0, tiled=True)
    receivers = sources
    for offset in range(1, rcv_count):
        moved = from_behind(sources, "src", -offset)
        receivers = jnp.where(rcv_place == offset, moved, receivers)
    scale = 1.0 / math.sqrt(sources.shape[0])
    lag_basis = lag_table()
    right = jnp.concatenate([receivers[..., :F], receivers[..., F:]], axis=0)
    row_block = min(64, block_rows)
    source_base = src_place * block_rows
    receiver_index = (src_place + rcv_place) * block_rows + jnp.arange(block_rows, dtype=jnp.int32)

    def one_rows(block_index):
        start = block_index * row_block
        chosen = lax.dynamic_slice_in_dim(sources, start, row_block, 1)
        src_real = chosen[..., :F]
        src_imag = chosen[..., F:]
        left = jnp.concatenate([src_real, src_imag], axis=0)
        left_imag = jnp.concatenate([src_imag, -src_real], axis=0)
        cross_real = jnp.einsum("kif,kjf->ijf", left, right, preferred_element_type=jnp.float32)
        cross_imag = jnp.einsum(
            "kif,kjf->ijf", left_imag, right, preferred_element_type=jnp.float32
        )
        stacked = (jnp.concatenate([cross_real, cross_imag], axis=2) * scale).astype(jnp.bfloat16)
        lagged = jnp.einsum("ijg,gc->ijc", stacked, lag_basis, preferred_element_type=jnp.float32)
        source_index = source_base + start + jnp.arange(row_block, dtype=jnp.int32)
        gap = receiver_index[None, :] - source_index[:, None]
        reach_rows = lax.dynamic_slice_in_dim(band_reach, start, row_block)
        keep = (gap >= 0) & (gap <= reach_rows[:, None])
        result = jnp.where(keep[:, :, None], lagged, 0.0).astype(jnp.bfloat16)
        return result.reshape(row_block, block_rows * LAGS)

    pieces = lax.map(one_rows, jnp.arange(block_rows // row_block, dtype=jnp.int32))
    return pieces.reshape(block_rows, block_rows * LAGS)


def solution(mesh):
    return jax.shard_map(
        body,
        mesh=mesh,
        in_specs=(P("rcv", "src", None), P("src"), P("src"), P("src"), P()),
        out_specs=P("src", "rcv"),
        check_vma=False,
    )
```

profile of v0, /device:TPU:10, one launch (start us, length us, event | category | flops | bytes accessed | tf_op | source)
XLA Modules:
  0.0 551.7 jit_solution(8811607649762527252)
XLA Ops:
  6.5 5.2 fusion.71
  13.0 3.6 fusion.40
  16.7 3.8 sort.17
  20.5 6.6 %copy.49 = f32[1536,1024]{0,1:T(8,128)} copy(f32[1536,1024]{1,0:T(8,128)} %get-tuple-element.128) | data formatting | bytes 12582912 | tf_op jit(solution)/shard_map/convert_element_type | solution.py:72
  40.2 6.2 %all-to-all-start = ((bf16[3,8,64,1,128]{4,2,0,3,1:T(8,128)(2,1)}), bf16[3,8,64,1,128]{4,2,0,3,1:T(8,128)(2,1)S(1)}, u32[]{:S(2)}, u32[]{:S(2)}) async-start(bf16[3,8,64,1,128]{4,2,0,3,1:T(8,128)(2,1)} %copy.53), calls=%async_computation | async-start | bytes 786432 | tf_op jit(solution)/shard_map/all_to_all | solution.py:101
  46.4 9.2 %all-to-all-done = bf16[3,8,64,1,128]{4,2,0,3,1:T(8,128)(2,1)S(1)} async-done(((bf16[3,8,64,1,128]{4,2,0,3,1:T(8,128)(2,1)}), bf16[3,8,64,1,128]{4,2,0,3,1:T(8,128)(2,1)S(1)}, u32[]{:S(2)}, u32[]{:S(2)}) %all-to-all-start) | async-done | bytes 393248 | tf_op jit(solution)/shard_map/all_to_all | solution.py:101
  56.6 20.9 %all-gather.2.cloned.1.call-done = bf16[12,512,128]{2,1,0:T(8,128)(2,1)} async-done(((bf16[3,512,128]{2,1,0:T(8,128)(2,1)}), bf16[12,512,128]{2,1,0:T(8,128)(2,1)}) %all-gather.2.cloned.1.call-update) | async-done | bytes 1572880 | tf_op jit(solution)/shard_map/all_gather | solution.py:106
  84.2 34.4 %collective-permute-done = bf16[12,512,128]{2,1,0:T(8,128)(2,1)S(1)} collective-permute-done((bf16[12,512,128]{2,1,0:T(8,128)(2,1)}, bf16[12,512,128]{2,1,0:T(8,128)(2,1)S(1)}, u32[]{:S(2)}, u32[]{:S(2)}) %collective-permute-start) | collective-permute-done | bytes 1572896 | tf_op jit(solution)/shard_map/ppermute | solution.py:22
  118.6 31.2 %collective-permute-done.1 = bf16[12,512,128]{2,1,0:T(8,128)(2,1)S(1)} collective-permute-done((bf16[12,512,128]{2,1,0:T(8,128)(2,1)}, bf16[12,512,128]{2,1,0:T(8,128)(2,1)S(1)}, u32[]{:S(2)}, u32[]{:S(2)}) %collective-permute-start.1) | collective-permute-done | bytes 1572896 | tf_op jit(solution)/shard_map/ppermute | solution.py:22
  149.9 68.4 %collective-permute-done.2 = bf16[12,512,128]{2,1,0:T(8,128)(2,1)} collective-permute-done((bf16[12,512,128]{2,1,0:T(8,128)(2,1)}, bf16[12,512,128]{2,1,0:T(8,128)(2,1)}, u32[]{:S(2)}, u32[]{:S(2)}) %collective-permute-start.2) | collective-permute-done | bytes 1572896 | tf_op jit(solution)/shard_map/ppermute | solution.py:22
  221.2 3.2 copy.56
  224.4 320.5 %while.11 = (s32[]{:T(128)}, bf16[8,64,16384]{2,1,0:T(8,128)(2,1)}, s32[8]{0:T(128)S(1)}, s32[]{:T(128)}, s32[512]{0:T(512)}, /*index=5*/bf16[12,512,128]{2,1,0:...) while((s32[]{:T(128)}, bf16[8,64,16384]{2,1,0:T(8,128)(2,1)}, ...), condition=%wide.region_3.4_spmd.clone, body=%wide.region_2.3_spmd.clone.sunk | while | flops 485409344 | bytes 69613544 | solution.py:138
  232.8 4.9 fusion.91
  238.6 13.1 %select_convert_fusion.2 = bf16[64,512,32]{1,2,0:T(8,128)(2,1)S(1)} fusion(pred[64,512]{1,0:T(8,128)(4,1)S(1)} %fusion.90, bf16[64,512,128]{1,0,2:T(8,128)(2,1)} %fusion.91, bf16[128,32]{0,1:T(8,128)(2,1)S(1)} %get-tuple-element.229), kind=kOutput, calls=%fused_computation.6.clone.1 | convolution fusion | flops 270532608 | bytes 10526720 | tf_op jit(solution)/shard_map/while/body/eval_jaxpr/ijg,gc->ijc/dot_general | solution.py:130
  251.6 7.8 %copy.81 = bf16[64,512,32]{0,2,1:T(8,128)(2,1)} copy(bf16[64,512,32]{1,2,0:T(8,128)(2,1)S(1)} %select_convert_fusion.2) | data formatting | bytes 4194304 | tf_op jit(solution)/shard_map/while/body/eval_jaxpr/convert_element_type | solution.py:135
  259.5 3.5 copy.82
  267.4 2.7 convolution_bitcast_fusion.5
  272.9 4.9 fusion.91
  278.6 13.1 %select_convert_fusion.2 = bf16[64,512,32]{1,2,0:T(8,128)(2,1)S(1)} fusion(pred[64,512]{1,0:T(8,128)(4,1)S(1)} %fusion.90, bf16[64,512,128]{1,0,2:T(8,128)(2,1)} %fusion.91, bf16[128,32]{0,1:T(8,128)(2,1)S(1)} %get-tuple-element.229), kind=kOutput, calls=%fused_computation.6.clone.1 | convolution fusion | flops 270532608 | bytes 10526720 | tf_op jit(solution)/shard_map/while/body/eval_jaxpr/ijg,gc->ijc/dot_general | solution.py:130
  291.7 7.8 %copy.81 = bf16[64,512,32]{0,2,1:T(8,128)(2,1)} copy(bf16[64,512,32]{1,2,0:T(8,128)(2,1)S(1)} %select_convert_fusion.2) | data formatting | bytes 4194304 | tf_op jit(solution)/shard_map/while/body/eval_jaxpr/convert_element_type | solution.py:135
  299.5 3.5 copy.82
  310.2 2.7 convolution_bitcast_fusion.4
  312.9 4.9 fusion.91
  318.7 13.1 %select_convert_fusion.2 = bf16[64,512,32]{1,2,0:T(8,128)(2,1)S(1)} fusion(pred[64,512]{1,0:T(8,128)(4,1)S(1)} %fusion.90, bf16[64,512,128]{1,0,2:T(8,128)(2,1)} %fusion.91, bf16[128,32]{0,1:T(8,128)(2,1)S(1)} %get-tuple-element.229), kind=kOutput, calls=%fused_computation.6.clone.1 | convolution fusion | flops 270532608 | bytes 10526720 | tf_op jit(solution)/shard_map/while/body/eval_jaxpr/ijg,gc->ijc/dot_general | solution.py:130
  331.7 7.8 %copy.81 = bf16[64,512,32]{0,2,1:T(8,128)(2,1)} copy(bf16[64,512,32]{1,2,0:T(8,128)(2,1)S(1)} %select_convert_fusion.2) | data formatting | bytes 4194304 | tf_op jit(solution)/shard_map/while/body/eval_jaxpr/convert_element_type | solution.py:135
  339.6 3.5 copy.82
  350.3 2.7 convolution_bitcast_fusion.4
  353.0 4.9 fusion.91
  358.7 13.1 %select_convert_fusion.2 = bf16[64,512,32]{1,2,0:T(8,128)(2,1)S(1)} fusion(pred[64,512]{1,0:T(8,128)(4,1)S(1)} %fusion.90, bf16[64,512,128]{1,0,2:T(8,128)(2,1)} %fusion.91, bf16[128,32]{0,1:T(8,128)(2,1)S(1)} %get-tuple-element.229), kind=kOutput, calls=%fused_computation.6.clone.1 | convolution fusion | flops 270532608 | bytes 10526720 | tf_op jit(solution)/shard_map/while/body/eval_jaxpr/ijg,gc->ijc/dot_general | solution.py:130
  371.8 7.8 %copy.81 = bf16[64,512,32]{0,2,1:T(8,128)(2,1)} copy(bf16[64,512,32]{1,2,0:T(8,128)(2,1)S(1)} %select_convert_fusion.2) | data formatting | bytes 4194304 | tf_op jit(solution)/shard_map/while/body/eval_jaxpr/convert_element_type | solution.py:135
  379.6 3.5 copy.82
  387.6 2.7 convolution_bitcast_fusion.5
  393.1 4.9 fusion.91
  398.8 13.1 %select_convert_fusion.2 = bf16[64,512,32]{1,2,0:T(8,128)(2,1)S(1)} fusion(pred[64,512]{1,0:T(8,128)(4,1)S(1)} %fusion.90, bf16[64,512,128]{1,0,2:T(8,128)(2,1)} %fusion.91, bf16[128,32]{0,1:T(8,128)(2,1)S(1)} %get-tuple-element.229), kind=kOutput, calls=%fused_computation.6.clone.1 | convolution fusion | flops 270532608 | bytes 10526720 | tf_op jit(solution)/shard_map/while/body/eval_jaxpr/ijg,gc->ijc/dot_general | solution.py:130
  411.9 7.8 %copy.81 = bf16[64,512,32]{0,2,1:T(8,128)(2,1)} copy(bf16[64,512,32]{1,2,0:T(8,128)(2,1)S(1)} %select_convert_fusion.2) | data formatting | bytes 4194304 | tf_op jit(solution)/shard_map/while/body/eval_jaxpr/convert_element_type | solution.py:135
  419.7 3.5 copy.82
  433.1 4.9 fusion.91
  438.9 13.1 %select_convert_fusion.2 = bf16[64,512,32]{1,2,0:T(8,128)(2,1)S(1)} fusion(pred[64,512]{1,0:T(8,128)(4,1)S(1)} %fusion.90, bf16[64,512,128]{1,0,2:T(8,128)(2,1)} %fusion.91, bf16[128,32]{0,1:T(8,128)(2,1)S(1)} %get-tuple-element.229), kind=kOutput, calls=%fused_computation.6.clone.1 | convolution fusion | flops 270532608 | bytes 10526720 | tf_op jit(solution)/shard_map/while/body/eval_jaxpr/ijg,gc->ijc/dot_general | solution.py:130
  451.9 7.8 %copy.81 = bf16[64,512,32]{0,2,1:T(8,128)(2,1)} copy(bf16[64,512,32]{1,2,0:T(8,128)(2,1)S(1)} %select_convert_fusion.2) | data formatting | bytes 4194304 | tf_op jit(solution)/shard_map/while/body/eval_jaxpr/convert_element_type | solution.py:135
  459.8 3.5 copy.82
  473.2 4.9 fusion.91
  478.9 13.1 %select_convert_fusion.2 = bf16[64,512,32]{1,2,0:T(8,128)(2,1)S(1)} fusion(pred[64,512]{1,0:T(8,128)(4,1)S(1)} %fusion.90, bf16[64,512,128]{1,0,2:T(8,128)(2,1)} %fusion.91, bf16[128,32]{0,1:T(8,128)(2,1)S(1)} %get-tuple-element.229), kind=kOutput, calls=%fused_computation.6.clone.1 | convolution fusion | flops 270532608 | bytes 10526720 | tf_op jit(solution)/shard_map/while/body/eval_jaxpr/ijg,gc->ijc/dot_general | solution.py:130
  492.0 7.8 %copy.81 = bf16[64,512,32]{0,2,1:T(8,128)(2,1)} copy(bf16[64,512,32]{1,2,0:T(8,128)(2,1)S(1)} %select_convert_fusion.2) | data formatting | bytes 4194304 | tf_op jit(solution)/shard_map/while/body/eval_jaxpr/convert_element_type | solution.py:135
  499.8 3.5 copy.82
  513.3 4.9 fusion.91
  519.0 13.1 %select_convert_fusion.2 = bf16[64,512,32]{1,2,0:T(8,128)(2,1)S(1)} fusion(pred[64,512]{1,0:T(8,128)(4,1)S(1)} %fusion.90, bf16[64,512,128]{1,0,2:T(8,128)(2,1)} %fusion.91, bf16[128,32]{0,1:T(8,128)(2,1)S(1)} %get-tuple-element.229), kind=kOutput, calls=%fused_computation.6.clone.1 | convolution fusion | flops 270532608 | bytes 10526720 | tf_op jit(solution)/shard_map/while/body/eval_jaxpr/ijg,gc->ijc/dot_general | solution.py:130
  532.1 7.8 %copy.81 = bf16[64,512,32]{0,2,1:T(8,128)(2,1)} copy(bf16[64,512,32]{1,2,0:T(8,128)(2,1)S(1)} %select_convert_fusion.2) | data formatting | bytes 4194304 | tf_op jit(solution)/shard_map/while/body/eval_jaxpr/convert_element_type | solution.py:135
  539.9 3.5 copy.82
  (150 shorter events, 94.5 us)
Async XLA Ops:
  13.0 3.7 copy-start.2
  27.0 2.8 copy-start
  28.3 3.0 slice-start
  29.8 2.0 slice-start.1
  34.3 0.8 copy-start.3
  35.9 10.5 %copy-start.1 = (s32[512]{0:T(512)S(1)}, s32[512]{0:T(512)}, u32[]{:S(2)}) copy-start(s32[512]{0:T(512)} %param.9) | copy-start | bytes 6148
  40.2 15.4 %all-to-all-start = ((bf16[3,8,64,1,128]{4,2,0,3,1:T(8,128)(2,1)}), bf16[3,8,64,1,128]{4,2,0,3,1:T(8,128)(2,1)S(1)}, u32[]{:S(2)}, u32[]{:S(2)}) async-start(bf16[3,8,64,1,128]{4,2,0,3,1:T(8,128)(2,1)} %copy.53), calls=%async_computation | async-start | bytes 786432 | tf_op jit(solution)/shard_map/all_to_all | solution.py:101
  46.4 31.1 %all-gather.2.cloned.1.call-start = ((), (), s32[]{:S(2)}) async-start(), calls=%async_computation.1 | async-start | bytes 1966080 | tf_op jit(solution)/shard_map/all_gather | solution.py:106
  77.5 41.2 %collective-permute-start = (bf16[12,512,128]{2,1,0:T(8,128)(2,1)}, bf16[12,512,128]{2,1,0:T(8,128)(2,1)S(1)}, u32[]{:S(2)}, u32[]{:S(2)}) collective-permute-start(bf16[12,512,128]{2,1,0:T(8,128)(2,1)} %all-gather.2.cloned.1.call-done), channel_id=1, source_target_pairs={{12,0},{16,4},{20,8},{24,12},{28,16},{13,1},{17,5},{21,9},{25,13},... | collective-permute-start | bytes 4718600 | tf_op jit(solution)/shard_map/ppermute | solution.py:22
  79.9 69.9 %collective-permute-start.1 = (bf16[12,512,128]{2,1,0:T(8,128)(2,1)}, bf16[12,512,128]{2,1,0:T(8,128)(2,1)S(1)}, u32[]{:S(2)}, u32[]{:S(2)}) collective-permute-start(bf16[12,512,128]{2,1,0:T(8,128)(2,1)} %all-gather.2.cloned.1.call-done), channel_id=1, source_target_pairs={{8,0},{12,4},{16,8},{20,12},{24,16},{28,20},{9,1},{13,5},{17,9},{2... | collective-permute-start | bytes 4718600 | tf_op jit(solution)/shard_map/ppermute | solution.py:22
  81.8 136.4 %collective-permute-start.2 = (bf16[12,512,128]{2,1,0:T(8,128)(2,1)}, bf16[12,512,128]{2,1,0:T(8,128)(2,1)}, u32[]{:S(2)}, u32[]{:S(2)}) collective-permute-start(bf16[12,512,128]{2,1,0:T(8,128)(2,1)} %all-gather.2.cloned.1.call-done), channel_id=1, source_target_pairs={{4,0},{8,4},{12,8},{16,12},{20,16},{24,20},{28,24},{5,1},{9,5},{13... | collective-permute-start | bytes 4718600 | tf_op jit(solution)/shard_map/ppermute | solution.py:22
Sparse Core Ops, SparseCore 0:
  56.7 20.6 all-gather.1
where the time goes:
time: 554 us; the launch traced here: 552 us
  waiting for transfers between devices  164 us (30%)
  matrix products  154 us (28%)
  local copies, waits for them, and re-layouts  144 us (26%)
  other arithmetic  57.7 us (10%)
  between operations  13.7 us (2%)
  starting transfers between devices  12.7 us (2%)
  loops' own time  5.66 us (1%)
    ppermute x3, waiting for transfers between devices, from_behind(): return lax.ppermute(block, axis, route)  134 us
    dot_general x8, matrix products, one_rows(): jnp.einsum('ijg,gc->ijc', stacked, lag_basis, preferred_element_type=jnp....  104 us
    convert_element_type x8, local copies, waits for them, and re-layouts, one_rows(): result = jnp.where(keep[:, :, None], lagged, 0.0).astype(jnp.bfloat16)  62.8 us
    dynamic_update_slice x16, local copies, waits for them, and re-layouts, body(): lax.map(one_rows, jnp.arange(block_rows // row_block, dtype=jnp.int32))  39.9 us
    convert_element_type x8, other arithmetic, one_rows(): (jnp.concatenate([cross_real, cross_imag], axis=2) * scale).astype(jnp.bf...  39 us
    dot_general x8, matrix products, one_rows(): jnp.einsum('kif,kjf->ijf', left, right, preferred_element_type=jnp.float32)  21.6 us
    dot_general x8, matrix products, one_rows(): jnp.einsum('kif,kjf->ijf', left_imag, right, preferred_element_type=jnp.f...  21.6 us
    all_gather x1, waiting for transfers between devices, body(): sources = lax.all_gather(own_block, 'rcv', axis=0, tiled=True)  20.9 us
  transfers between devices with their start and end apart: 5, of which 5 were waited for; matrix products, arithmetic and copies ran while one was open for 0% of the time, Pallas kernels for 0%

commit v1 on v0

v1 whole, which is shorter than its diff:
```python
import functools
import math

import jax
import jax.numpy as jnp
import ml_dtypes
import numpy as np
from jax import lax
from jax.experimental import pallas as pl
from jax.experimental.pallas import tpu as pltpu
from jax.sharding import PartitionSpec as P

F = 64
K0 = 32
HW = 64
LAGS = 32
CHUNK = 16

norm_floor = 1e-05
water_level = 0.3


def basis_table(length):
    sample_index = np.arange(length)
    bin_index = np.arange(F) + K0
    phase = np.mod(sample_index[:, None] * bin_index[None, :], length)
    angle = phase * (2.0 * math.pi / length)
    table = np.concatenate([np.cos(angle), -np.sin(angle)], axis=1)
    return table.astype(np.float32).astype(ml_dtypes.bfloat16)


def lag_tables(length):
    bin_index = np.arange(F) + K0
    lag_index = np.arange(LAGS) - LAGS // 2
    phase = np.mod(lag_index[:, None] * bin_index[None, :], length)
    angle = phase * (2.0 * math.pi / length)
    scale = 1.0 / math.sqrt(F)
    cosine = (np.cos(angle) * scale).astype(np.float32).astype(ml_dtypes.bfloat16)
    sine = (np.sin(angle) * scale).astype(np.float32).astype(ml_dtypes.bfloat16)
    straight = np.concatenate([cosine, cosine], axis=1).astype(np.float32)
    swapped = np.concatenate([-sine, sine], axis=1).astype(np.float32)
    return straight, swapped


def inverse_counts(length):
    positions = np.arange(length)
    upper = np.minimum(positions + HW, length - 1)
    lower = np.maximum(positions - HW, 0)
    return (1.0 / (upper - lower + 1)).astype(np.float32)[None, :]


def band(rows, columns, shift):
    row = lax.broadcasted_iota(jnp.int32, (rows, columns), 0)
    column = lax.broadcasted_iota(jnp.int32, (rows, columns), 1)
    return (jnp.abs(row - column - shift) <= HW).astype(jnp.float32).astype(jnp.bfloat16)


def whiten_kernel(src_count, x_ref, channel_ref, taper_ref, inverse_ref, basis_ref, out_ref, normed_ref):
    samples = x_ref[0]
    rows, length = samples.shape
    width = 256
    for start in range(0, length, width):
        low = max(start - 128, 0)
        high = min(start + width + 128, length)
        magnitude = jnp.abs(x_ref[0, :, low:high])
        total = jnp.dot(
            magnitude, band(high - low, width, start - low), preferred_element_type=jnp.float32
        )
        level = total * inverse_ref[:, start : start + width] + norm_floor
        values = x_ref[0, :, start : start + width].astype(jnp.float32)
        normed_ref[:, start : start + width] = (values / level).astype(jnp.bfloat16)
    spectrum = jnp.dot(normed_ref[...], basis_ref[...], preferred_element_type=jnp.float32)
    square = spectrum * spectrum
    amplitude = jnp.sqrt(square + pltpu.roll(square, F, 1))
    bins = lax.broadcasted_iota(jnp.int32, (1, 2 * F), 1) % F
    first, last = bins == 0, bins == F - 1
    below = jnp.where(first, 0.0, pltpu.roll(amplitude, 1, 1))
    above = jnp.where(last, 0.0, pltpu.roll(amplitude, 2 * F - 1, 1))
    share = jnp.where(first | last, 1.0 / 2.0, 1.0 / 3.0)
    smooth = (below + amplitude + above) * share
    mean = jnp.sum(amplitude, axis=1, keepdims=True) * (0.5 / F)
    level = jnp.maximum(smooth, water_level * (mean + norm_floor))
    white = (spectrum * (taper_ref[...] / level)).astype(jnp.bfloat16)
    floor = lax.broadcasted_iota(jnp.int32, (rows, rows), 0) * src_count
    channel = channel_ref[...]
    pick = (channel >= floor) & (channel < floor + src_count)
    pick = pick.astype(jnp.float32).astype(jnp.bfloat16)
    ordered = jnp.dot(pick, white, preferred_element_type=jnp.float32).astype(jnp.bfloat16)
    out_ref[:, 0] = ordered.reshape(src_count, rows // src_count, 2 * F)


def whiten(raw_samples, channel_of_row, bin_taper, src_count):
    windows, rows, length = raw_samples.shape
    part = rows // src_count
    whole = lambda *shape: pl.BlockSpec(shape, lambda w: (0,) * len(shape))
    return pl.pallas_call(
        functools.partial(whiten_kernel, src_count),
        grid=(windows,),
        out_shape=jax.ShapeDtypeStruct((src_count, windows, part, 2 * F), jnp.bfloat16),
        in_specs=[
            pl.BlockSpec((1, rows, length), lambda w: (w, 0, 0)),
            whole(1, rows),
            whole(1, 2 * F),
            whole(1, length),
            whole(length, 2 * F),
        ],
        out_specs=pl.BlockSpec((src_count, 1, part, 2 * F), lambda w: (0, w, 0, 0)),
        scratch_shapes=[pltpu.VMEM((rows, length), jnp.bfloat16)],
        compiler_params=pltpu.CompilerParams(vmem_limit_bytes=40 << 20),
        name="whiten",
    )(
        raw_samples,
        channel_of_row.reshape(1, rows),
        jnp.tile(bin_taper, 2).reshape(1, 2 * F),
        jnp.asarray(inverse_counts(length)),
        jnp.asarray(basis_table(length)),
    )


def correlate_kernel(pieces, windows, scale, *refs):
    src_refs, rcv_refs = refs[:pieces], refs[pieces : 2 * pieces]
    reach_ref, straight_ref, swapped_ref, out_ref = refs[2 * pieces : 2 * pieces + 4]
    left_ref, rcv_ref, turned_ref, even_ref, odd_ref = refs[2 * pieces + 4 :]
    step = pl.program_id(0)
    src_count, local, part, lanes = src_refs[0].shape
    rows = src_count * part
    columns = CHUNK * LAGS

    def rotate(first, target):
        straight = straight_ref[...][None]
        swapped = swapped_ref[...][None]
        for w in range(windows):
            plain = rcv_ref[w, pl.ds(first, CHUNK), :]
            turned = turned_ref[w, pl.ds(first, CHUNK), :]
            value = plain[:, None, :] * straight + turned[:, None, :] * swapped
            target[:, w * lanes : (w + 1) * lanes] = value.reshape(columns, lanes).astype(
                jnp.bfloat16
            )

    @pl.when(step == 0)
    def _():
        natural = lax.broadcasted_iota(jnp.int32, (rows, rows), 0)
        held = lax.broadcasted_iota(jnp.int32, (rows, rows), 1)
        pick = natural == (held % part) * src_count + held // part
        pick = pick.astype(jnp.float32).astype(jnp.bfloat16)
        for d in range(pieces):
            for n in range(local):
                w = d * local + n
                block = src_refs[d][:, n].reshape(rows, lanes)
                left_ref[:, w * lanes : (w + 1) * lanes] = jnp.dot(
                    pick, block, preferred_element_type=jnp.float32
                ).astype(jnp.bfloat16)
                block = rcv_refs[d][:, n].reshape(rows, lanes)
                value = jnp.dot(pick, block, preferred_element_type=jnp.float32)
                rcv_ref[w] = value
                turned_ref[w] = pltpu.roll(value, F, 1)
        rotate(0, even_ref)

    shift = lax.axis_index("rcv") * rows
    low = (lax.broadcasted_iota(jnp.int32, (rows, 1), 0) - shift) * LAGS
    high = low + reach_ref[...] * LAGS + (LAGS - 1)

    def multiply(source, half):
        total = lax.dot_general(
            left_ref[...], source[...], (((1,), (1,)), ((), ())), preferred_element_type=jnp.float32
        )
        column = lax.broadcasted_iota(jnp.int32, (1, columns), 1)
        column = column + (2 * step + half) * columns
        keep = (column >= low) & (column <= high)
        out_ref[:, half * columns : (half + 1) * columns] = jnp.where(
            keep, total * scale, 0.0
        ).astype(jnp.bfloat16)

    multiply(even_ref, 0)
    rotate((2 * step + 1) * CHUNK, odd_ref)
    multiply(odd_ref, 1)
    rotate(jnp.minimum(2 * step + 2, rows // CHUNK - 1) * CHUNK, even_ref)


def correlate(src_pieces, rcv_pieces, band_reach, length):
    pieces = len(src_pieces)
    src_count, local, part, lanes = src_pieces[0].shape
    rows = src_count * part
    windows = pieces * local
    straight, swapped = lag_tables(length)
    whole = lambda *shape: pl.BlockSpec(shape, lambda g: (0,) * len(shape))
    columns = CHUNK * LAGS
    depth = windows * lanes
    return pl.pallas_call(
        functools.partial(correlate_kernel, pieces, windows, 1.0 / math.sqrt(windows)),
        grid=(rows // (2 * CHUNK),),
        out_shape=jax.ShapeDtypeStruct((rows, rows * LAGS), jnp.bfloat16),
        in_specs=[whole(src_count, local, part, lanes)] * (2 * pieces)
        + [whole(rows, 1), whole(LAGS, lanes), whole(LAGS, lanes)],
        out_specs=pl.BlockSpec((rows, 2 * columns), lambda g: (0, g)),
        scratch_shapes=[
            pltpu.VMEM((rows, depth), jnp.bfloat16),
            pltpu.VMEM((windows, rows, lanes), jnp.float32),
            pltpu.VMEM((windows, rows, lanes), jnp.float32),
            pltpu.VMEM((columns, depth), jnp.bfloat16),
            pltpu.VMEM((columns, depth), jnp.bfloat16),
        ],
        compiler_params=pltpu.CompilerParams(vmem_limit_bytes=56 << 20),
        name="correlate",
    )(
        *src_pieces,
        *rcv_pieces,
        band_reach.reshape(rows, 1),
        jnp.asarray(straight),
        jnp.asarray(swapped),
    )


def body(raw_samples, channel_of_row, live_channels, band_reach, bin_taper):
    src_count = lax.axis_size("src")
    rcv_count = lax.axis_size("rcv")
    windows, rows, length = raw_samples.shape
    part = rows // src_count
    ordered = whiten(raw_samples, channel_of_row, bin_taper, src_count)
    arrived = lax.all_to_all(ordered, "src", split_axis=0, concat_axis=0, tiled=True)
    live = live_channels.reshape(part, src_count).T.astype(jnp.bfloat16)
    own = arrived * live[:, None, :, None]
    src_pieces, rcv_pieces = [own], []
    for d in range(rcv_count):
        if d:
            route = [(i, (i + d) % rcv_count) for i in range(rcv_count)]
            src_pieces.append(lax.ppermute(own, "rcv", route))
        route = []
        for s in range(src_count):
            for r in range(rcv_count):
                to = (r + d) % rcv_count
                if s >= to:
                    route.append((s * rcv_count + r, (s - to) * rcv_count + to))
        rcv_pieces.append(lax.ppermute(own, ("src", "rcv"), route))
    return correlate(src_pieces, rcv_pieces, band_reach, length)


def solution(mesh):
    return jax.shard_map(
        body,
        mesh=mesh,
        in_specs=(P("rcv", "src", None), P("src"), P("src"), P("src"), P()),
        out_specs=P("src", "rcv"),
        check_vma=False,
    )
```

time: 554 us -> 119 us (0.21)
  the two profiles are of different devices: /device:TPU:10 before, /device:TPU:6 now
where the time goes in v1:
time: 119 us; the launch traced here: 118 us
  Pallas kernels  51.1 us (43%)
  waiting for transfers between devices  43.8 us (37%)
  starting transfers between devices  14.9 us (13%)
  local copies, waits for them, and re-layouts  7.41 us (6%)
    pallas_call x1, Pallas kernels, correlate(): pl.pallas_call(functools.partial(correlate_kernel, pieces, windows, 1.0 /...  43.1 us
    ppermute x4, waiting for transfers between devices, body(): rcv_pieces.append(lax.ppermute(own, ('src', 'rcv'), route))  17 us
    ppermute x3, waiting for transfers between devices, body(): src_pieces.append(lax.ppermute(own, 'rcv', route))  16.6 us
    all_to_all x1, waiting for transfers between devices, body(): lax.all_to_all(ordered, 'src', split_axis=0, concat_axis=0, tiled=True)  10.3 us
    pallas_call x1, Pallas kernels, whiten(): pl.pallas_call(functools.partial(whiten_kernel, src_count), grid=(windows...  7.95 us
    ppermute x4, starting transfers between devices, body(): rcv_pieces.append(lax.ppermute(own, ('src', 'rcv'), route))  6.43 us
    all_to_all x1, starting transfers between devices, body(): lax.all_to_all(ordered, 'src', split_axis=0, concat_axis=0, tiled=True)  6.34 us
    unnamed x24, local copies, waits for them, and re-layouts  4.97 us
  transfers between devices with their start and end apart: 8, of which 5 were waited for; matrix products, arithmetic and copies ran while one was open for 2% of the time, Pallas kernels for 0%

profile of v1, /device:TPU:6, one launch (start us, length us, event | category | flops | bytes accessed | tf_op | source)
XLA Modules:
  0.0 118.1 jit_solution(18409813711984130314)
XLA Ops:
  0.0 0.7 tile.2
  0.7 0.1 reshape_tile.3.taper_ref
  0.7 0.0 copy-start
  0.7 1.9 %copy-done = bf16[3,512,1024]{2,1,0:T(8,128)(2,1)S(1)} copy-done((bf16[3,512,1024]{2,1,0:T(8,128)(2,1)S(1)}, bf16[3,512,1024]{2,1,0:T(8,128)(2,1)}, u32[]{:S(2)}) %copy-start) | copy-done | bytes 3145752
  2.6 0.0 copy-start.1
  2.6 0.9 copy-done.1
  3.6 0.0 copy-start.2
  3.6 0.7 copy-done.2
  4.3 0.7 copy-done.3
  5.0 7.9 %whiten.1 = bf16[8,3,64,128]{3,2,1,0:T(8,128)(2,1)} custom-call(bf16[3,512,1024]{2,1,0:T(8,128)(2,1)S(1)} %copy-done, s32[1,512]{1,0:T(1,128)S(1)} %bitcast.3, f32[1,128]{1,0:T(1,128)S(1)} %reshape_tile.3.taper_ref, f32[1,1024]{1,0:T(1,128)S(1)} %copy-done.2, bf16[1024,128]{1,0:T(8,128)(2,1)S(1)} %copy-done.1), custom_call_target="tpu_custom_call" | custom-call | tf_op jit(solution)/shard_map/whiten/pallas_call | solution.py:96
  12.9 6.3 %all-to-all-start = ((bf16[8,3,64,128]{3,2,1,0:T(8,128)(2,1)}), bf16[8,3,64,128]{3,2,1,0:T(8,128)(2,1)S(1)}, u32[]{:S(2)}, u32[]{:S(2)}) async-start(bf16[8,3,64,128]{3,2,1,0:T(8,128)(2,1)} %whiten.1), calls=%async_computation | async-start | bytes 786432 | tf_op jit(solution)/shard_map/all_to_all | solution.py:220
  19.2 0.7 convert_element_type.9
  19.9 0.1 convert_element_type.10
  20.0 0.1 copy.10
  20.1 10.3 %all-to-all-done = bf16[8,3,64,128]{3,2,1,0:T(8,128)(2,1)S(1)} async-done(((bf16[8,3,64,128]{3,2,1,0:T(8,128)(2,1)}), bf16[8,3,64,128]{3,2,1,0:T(8,128)(2,1)S(1)}, u32[]{:S(2)}, u32[]{:S(2)}) %all-to-all-start) | async-done | bytes 393248 | tf_op jit(solution)/shard_map/all_to_all | solution.py:220
  30.4 0.1 broadcast_multiply_fusion.refs_0_
  30.5 0.0 copy-start.4
  30.5 1.9 %collective-permute-start.6 = (bf16[8,3,64,128]{3,2,1,0:T(8,128)(2,1)S(1)}, bf16[8,3,64,128]{3,2,1,0:T(8,128)(2,1)S(1)}, u32[]{:S(2)}, u32[]{:S(2)}) collective-permute-start(bf16[8,3,64,128]{3,2,1,0:T(8,128)(2,1)S(1)} %broadcast_multiply_fusion.refs_0_), channel_id=1, source_target_pairs={{1,0},{5,4},{6,1},{9,8},{10,5},{11,2},{12,3},{13,12},{14,9},{15,6}... | collective-permute-start | bytes 1179656 | tf_op jit(solution)/shard_map/ppermute | solution.py:234
  32.4 1.9 %collective-permute-start.5 = (bf16[8,3,64,128]{3,2,1,0:T(8,128)(2,1)S(1)}, bf16[8,3,64,128]{3,2,1,0:T(8,128)(2,1)S(1)}, u32[]{:S(2)}, u32[]{:S(2)}) collective-permute-start(bf16[8,3,64,128]{3,2,1,0:T(8,128)(2,1)S(1)} %broadcast_multiply_fusion.refs_0_), channel_id=1, source_target_pairs={{2,0},{6,4},{7,1},{8,2},{10,8},{11,5},{12,6},{13,3},{14,12},{15,9}... | collective-permute-start | bytes 1179656 | tf_op jit(solution)/shard_map/ppermute | solution.py:234
  34.4 1.3 %collective-permute-start.4 = (bf16[8,3,64,128]{3,2,1,0:T(8,128)(2,1)S(1)}, bf16[8,3,64,128]{3,2,1,0:T(8,128)(2,1)S(1)}, u32[]{:S(2)}, u32[]{:S(2)}) collective-permute-start(bf16[8,3,64,128]{3,2,1,0:T(8,128)(2,1)S(1)} %broadcast_multiply_fusion.refs_0_), channel_id=1, source_target_pairs={{3,0},{4,1},{7,4},{8,5},{9,2},{11,8},{12,9},{13,6},{14,3},{15,12},... | collective-permute-start | bytes 1179656 | tf_op jit(solution)/shard_map/ppermute | solution.py:234
  35.7 1.3 %collective-permute-start.3 = (bf16[8,3,64,128]{3,2,1,0:T(8,128)(2,1)S(1)}, bf16[8,3,64,128]{3,2,1,0:T(8,128)(2,1)S(1)}, u32[]{:S(2)}, u32[]{:S(2)}) collective-permute-start(bf16[8,3,64,128]{3,2,1,0:T(8,128)(2,1)S(1)} %broadcast_multiply_fusion.refs_0_), channel_id=1, source_target_pairs={{0,0},{4,4},{5,1},{8,8},{9,5},{10,2},{12,12},{13,9},{14,6},{15,3},... | collective-permute-start | bytes 1179656 | tf_op jit(solution)/shard_map/ppermute | solution.py:234
  37.0 0.9 collective-permute-start.2
  37.9 8.2 %collective-permute-done.6.refs_7_ = bf16[8,3,64,128]{3,2,1,0:T(8,128)(2,1)S(1)} collective-permute-done((bf16[8,3,64,128]{3,2,1,0:T(8,128)(2,1)S(1)}, bf16[8,3,64,128]{3,2,1,0:T(8,128)(2,1)S(1)}, u32[]{:S(2)}, u32[]{:S(2)}) %collective-permute-start.6) | collective-permute-done | bytes 393248 | tf_op jit(solution)/shard_map/ppermute | solution.py:234
  46.1 0.0 copy-start.5
  46.1 0.0 collective-permute-start.1
  46.1 8.7 %collective-permute-done.5.refs_6_ = bf16[8,3,64,128]{3,2,1,0:T(8,128)(2,1)S(1)} collective-permute-done((bf16[8,3,64,128]{3,2,1,0:T(8,128)(2,1)S(1)}, bf16[8,3,64,128]{3,2,1,0:T(8,128)(2,1)S(1)}, u32[]{:S(2)}, u32[]{:S(2)}) %collective-permute-start.5) | collective-permute-done | bytes 393248 | tf_op jit(solution)/shard_map/ppermute | solution.py:234
  54.9 0.0 copy-start.6
  54.9 1.2 collective-permute-start
  56.0 1.5 %copy.11.refs_8_ = s32[512,1]{1,0:T(8,128)} copy(s32[512,1]{0,1:T(1,128)} %bitcast.5) | data formatting | bytes 4096 | tf_op jit(solution)/shard_map/reshape | solution.py:208
  57.6 0.0 collective-permute-done.4.refs_5_
  57.6 0.0 copy-start.7
  57.6 0.0 collective-permute-done.3.refs_4_
  57.6 0.0 copy-start.8
  57.6 0.0 collective-permute-done.2.refs_3_
  57.6 0.0 copy-start.9
  57.6 15.3 %collective-permute-done.1.refs_2_ = bf16[8,3,64,128]{3,2,1,0:T(8,128)(2,1)S(1)} collective-permute-done((bf16[8,3,64,128]{3,2,1,0:T(8,128)(2,1)S(1)}, bf16[8,3,64,128]{3,2,1,0:T(8,128)(2,1)S(1)}, u32[]{:S(2)}, u32[]{:S(2)}) %collective-permute-start.1) | collective-permute-done | bytes 393248 | tf_op jit(solution)/shard_map/ppermute | solution.py:227
  72.9 0.0 copy-start.10
  72.9 1.3 %collective-permute-done.refs_1_ = bf16[8,3,64,128]{3,2,1,0:T(8,128)(2,1)S(1)} collective-permute-done((bf16[8,3,64,128]{3,2,1,0:T(8,128)(2,1)S(1)}, bf16[8,3,64,128]{3,2,1,0:T(8,128)(2,1)S(1)}, u32[]{:S(2)}, u32[]{:S(2)}) %collective-permute-start) | collective-permute-done | bytes 393248 | tf_op jit(solution)/shard_map/ppermute | solution.py:227
  74.2 0.0 copy-done.4
  74.2 0.0 copy-done.5
  74.2 0.0 copy-done.6
  74.2 0.0 copy-done.7
  74.2 0.0 copy-done.8
  74.2 0.0 copy-done.9
  74.2 0.0 copy-done.10
  74.2 0.0 copy-start.11
  74.2 0.7 copy-done.11
  75.0 43.1 %correlate.1 = bf16[512,16384]{1,0:T(8,128)(2,1)} custom-call(bf16[8,3,64,128]{3,2,1,0:T(8,128)(2,1)} %copy-done.4, bf16[8,3,64,128]{3,2,1,0:T(8,128)(2,1)} %copy-done.11, bf16[8,3,64,128]{3,2,1,0:T(8,128)(2,1)} %copy-done.10, bf16[8,3,64,128]{3,2,1,0:T(8,128)(2,1)} %copy-done.9, bf16[8,3,64,128]{3,2,1,0:T(8,128)(2,1)} %copy-done.8, ...), custom_call_target="tpu_custom_call" | custom-call | tf_op jit(solution)/shard_map/correlate/pallas_call | solution.py:189
  (1 shorter events, 0.0 us)
Async XLA Ops:
  0.7 1.9 %copy-start = (bf16[3,512,1024]{2,1,0:T(8,128)(2,1)S(1)}, bf16[3,512,1024]{2,1,0:T(8,128)(2,1)}, u32[]{:S(2)}) copy-start(bf16[3,512,1024]{2,1,0:T(8,128)(2,1)} %x_ref.1) | copy-start | bytes 9437188
  2.6 0.9 copy-start.1
  3.6 0.7 copy-start.2
  4.3 0.7 copy-start.3
  12.9 17.5 %all-to-all-start = ((bf16[8,3,64,128]{3,2,1,0:T(8,128)(2,1)}), bf16[8,3,64,128]{3,2,1,0:T(8,128)(2,1)S(1)}, u32[]{:S(2)}, u32[]{:S(2)}) async-start(bf16[8,3,64,128]{3,2,1,0:T(8,128)(2,1)} %whiten.1), calls=%async_computation | async-start | bytes 786432 | tf_op jit(solution)/shard_map/all_to_all | solution.py:220
  30.5 43.7 %copy-start.4 = (bf16[8,3,64,128]{3,2,1,0:T(8,128)(2,1)}, bf16[8,3,64,128]{3,2,1,0:T(8,128)(2,1)S(1)}, u32[]{:S(2)}) copy-start(bf16[8,3,64,128]{3,2,1,0:T(8,128)(2,1)S(1)} %broadcast_multiply_fusion.refs_0_) | copy-start | bytes 1179652
  30.5 15.6 %collective-permute-start.6 = (bf16[8,3,64,128]{3,2,1,0:T(8,128)(2,1)S(1)}, bf16[8,3,64,128]{3,2,1,0:T(8,128)(2,1)S(1)}, u32[]{:S(2)}, u32[]{:S(2)}) collective-permute-start(bf16[8,3,64,128]{3,2,1,0:T(8,128)(2,1)S(1)} %broadcast_multiply_fusion.refs_0_), channel_id=1, source_target_pairs={{1,0},{5,4},{6,1},{9,8},{10,5},{11,2},{12,3},{13,12},{14,9},{15,6}... | collective-permute-start | bytes 1179656 | tf_op jit(solution)/shard_map/ppermute | solution.py:234
  32.4 22.4 %collective-permute-start.5 = (bf16[8,3,64,128]{3,2,1,0:T(8,128)(2,1)S(1)}, bf16[8,3,64,128]{3,2,1,0:T(8,128)(2,1)S(1)}, u32[]{:S(2)}, u32[]{:S(2)}) collective-permute-start(bf16[8,3,64,128]{3,2,1,0:T(8,128)(2,1)S(1)} %broadcast_multiply_fusion.refs_0_), channel_id=1, source_target_pairs={{2,0},{6,4},{7,1},{8,2},{10,8},{11,5},{12,6},{13,3},{14,12},{15,9}... | collective-permute-start | bytes 1179656 | tf_op jit(solution)/shard_map/ppermute | solution.py:234
  34.4 23.2 %collective-permute-start.4 = (bf16[8,3,64,128]{3,2,1,0:T(8,128)(2,1)S(1)}, bf16[8,3,64,128]{3,2,1,0:T(8,128)(2,1)S(1)}, u32[]{:S(2)}, u32[]{:S(2)}) collective-permute-start(bf16[8,3,64,128]{3,2,1,0:T(8,128)(2,1)S(1)} %broadcast_multiply_fusion.refs_0_), channel_id=1, source_target_pairs={{3,0},{4,1},{7,4},{8,5},{9,2},{11,8},{12,9},{13,6},{14,3},{15,12},... | collective-permute-start | bytes 1179656 | tf_op jit(solution)/shard_map/ppermute | solution.py:234
  35.7 21.9 %collective-permute-start.3 = (bf16[8,3,64,128]{3,2,1,0:T(8,128)(2,1)S(1)}, bf16[8,3,64,128]{3,2,1,0:T(8,128)(2,1)S(1)}, u32[]{:S(2)}, u32[]{:S(2)}) collective-permute-start(bf16[8,3,64,128]{3,2,1,0:T(8,128)(2,1)S(1)} %broadcast_multiply_fusion.refs_0_), channel_id=1, source_target_pairs={{0,0},{4,4},{5,1},{8,8},{9,5},{10,2},{12,12},{13,9},{14,6},{15,3},... | collective-permute-start | bytes 1179656 | tf_op jit(solution)/shard_map/ppermute | solution.py:234
  37.0 20.6 %collective-permute-start.2 = (bf16[8,3,64,128]{3,2,1,0:T(8,128)(2,1)S(1)}, bf16[8,3,64,128]{3,2,1,0:T(8,128)(2,1)S(1)}, u32[]{:S(2)}, u32[]{:S(2)}) collective-permute-start(bf16[8,3,64,128]{3,2,1,0:T(8,128)(2,1)S(1)} %broadcast_multiply_fusion.refs_0_), channel_id=1, source_target_pairs={{0,3},{1,0},{2,1},{3,2},{4,7},{5,4},{6,5},{7,6},{8,11},{9,8},{10,9... | collective-permute-start | bytes 1179656 | tf_op jit(solution)/shard_map/ppermute | solution.py:227
  46.1 28.0 %copy-start.5 = (bf16[8,3,64,128]{3,2,1,0:T(8,128)(2,1)}, bf16[8,3,64,128]{3,2,1,0:T(8,128)(2,1)S(1)}, u32[]{:S(2)}) copy-start(bf16[8,3,64,128]{3,2,1,0:T(8,128)(2,1)S(1)} %collective-permute-done.6.refs_7_) | copy-start | bytes 1179652
  46.1 26.8 %collective-permute-start.1 = (bf16[8,3,64,128]{3,2,1,0:T(8,128)(2,1)S(1)}, bf16[8,3,64,128]{3,2,1,0:T(8,128)(2,1)S(1)}, u32[]{:S(2)}, u32[]{:S(2)}) collective-permute-start(bf16[8,3,64,128]{3,2,1,0:T(8,128)(2,1)S(1)} %broadcast_multiply_fusion.refs_0_), channel_id=1, source_target_pairs={{0,2},{1,3},{2,0},{3,1},{4,6},{5,7},{6,4},{7,5},{8,10},{9,11},{10,... | collective-permute-start | bytes 1179656 | tf_op jit(solution)/shard_map/ppermute | solution.py:227
  54.9 19.3 %copy-start.6 = (bf16[8,3,64,128]{3,2,1,0:T(8,128)(2,1)}, bf16[8,3,64,128]{3,2,1,0:T(8,128)(2,1)S(1)}, u32[]{:S(2)}) copy-start(bf16[8,3,64,128]{3,2,1,0:T(8,128)(2,1)S(1)} %collective-permute-done.5.refs_6_) | copy-start | bytes 1179652
  54.9 19.3 %collective-permute-start = (bf16[8,3,64,128]{3,2,1,0:T(8,128)(2,1)S(1)}, bf16[8,3,64,128]{3,2,1,0:T(8,128)(2,1)S(1)}, u32[]{:S(2)}, u32[]{:S(2)}) collective-permute-start(bf16[8,3,64,128]{3,2,1,0:T(8,128)(2,1)S(1)} %broadcast_multiply_fusion.refs_0_), channel_id=1, source_target_pairs={{0,1},{1,2},{2,3},{3,0},{4,5},{5,6},{6,7},{7,4},{8,9},{9,10},{10,1... | collective-permute-start | bytes 1179656 | tf_op jit(solution)/shard_map/ppermute | solution.py:227
  57.6 16.6 %copy-start.7 = (bf16[8,3,64,128]{3,2,1,0:T(8,128)(2,1)}, bf16[8,3,64,128]{3,2,1,0:T(8,128)(2,1)S(1)}, u32[]{:S(2)}) copy-start(bf16[8,3,64,128]{3,2,1,0:T(8,128)(2,1)S(1)} %collective-permute-done.4.refs_5_) | copy-start | bytes 1179652
  57.6 16.6 %copy-start.8 = (bf16[8,3,64,128]{3,2,1,0:T(8,128)(2,1)}, bf16[8,3,64,128]{3,2,1,0:T(8,128)(2,1)S(1)}, u32[]{:S(2)}) copy-start(bf16[8,3,64,128]{3,2,1,0:T(8,128)(2,1)S(1)} %collective-permute-done.3.refs_4_) | copy-start | bytes 1179652
  57.6 16.6 %copy-start.9 = (bf16[8,3,64,128]{3,2,1,0:T(8,128)(2,1)}, bf16[8,3,64,128]{3,2,1,0:T(8,128)(2,1)S(1)}, u32[]{:S(2)}) copy-start(bf16[8,3,64,128]{3,2,1,0:T(8,128)(2,1)S(1)} %collective-permute-done.2.refs_3_) | copy-start | bytes 1179652
  72.9 1.3 %copy-start.10 = (bf16[8,3,64,128]{3,2,1,0:T(8,128)(2,1)}, bf16[8,3,64,128]{3,2,1,0:T(8,128)(2,1)S(1)}, u32[]{:S(2)}) copy-start(bf16[8,3,64,128]{3,2,1,0:T(8,128)(2,1)S(1)} %collective-permute-done.1.refs_2_) | copy-start | bytes 1179652
  74.2 0.7 copy-start.11

commit v2 on v1

v2 whole, which is shorter than its diff:
```python
import functools
import math

import jax
import jax.numpy as jnp
import ml_dtypes
import numpy as np
from jax import lax
from jax.experimental import pallas as pl
from jax.experimental.pallas import tpu as pltpu
from jax.sharding import PartitionSpec as P

F = 64
K0 = 32
HW = 64
LAGS = 32
CHUNK = 16

norm_floor = 1e-05
water_level = 0.3


def basis_table(length):
    sample_index = np.arange(length)
    bin_index = np.arange(F) + K0
    phase = np.mod(sample_index[:, None] * bin_index[None, :], length)
    angle = phase * (2.0 * math.pi / length)
    table = np.concatenate([np.cos(angle), -np.sin(angle)], axis=1)
    return table.astype(np.float32).astype(ml_dtypes.bfloat16)


def lag_tables(length):
    bin_index = np.arange(F) + K0
    lag_index = np.arange(LAGS) - LAGS // 2
    phase = np.mod(lag_index[:, None] * bin_index[None, :], length)
    angle = phase * (2.0 * math.pi / length)
    scale = 1.0 / math.sqrt(F)
    cosine = (np.cos(angle) * scale).astype(np.float32).astype(ml_dtypes.bfloat16)
    sine = (np.sin(angle) * scale).astype(np.float32).astype(ml_dtypes.bfloat16)
    straight = np.concatenate([cosine, cosine], axis=1).astype(np.float32)
    swapped = np.concatenate([-sine, sine], axis=1).astype(np.float32)
    return straight, swapped


def inverse_counts(length):
    positions = np.arange(length)
    upper = np.minimum(positions + HW, length - 1)
    lower = np.maximum(positions - HW, 0)
    return (1.0 / (upper - lower + 1)).astype(np.float32)[None, :]


def band(rows, columns, shift):
    row = lax.broadcasted_iota(jnp.int32, (rows, columns), 0)
    column = lax.broadcasted_iota(jnp.int32, (rows, columns), 1)
    return (jnp.abs(row - column - shift) <= HW).astype(jnp.float32).astype(jnp.bfloat16)


def whiten_window(w, src_count, x_ref, channel_ref, taper_ref, inverse_ref, basis_ref, normed_ref):
    rows, length = x_ref.shape[1:]
    width = 256
    for start in range(0, length, width):
        low = max(start - 128, 0)
        high = min(start + width + 128, length)
        magnitude = jnp.abs(x_ref[w, :, low:high])
        total = jnp.dot(
            magnitude, band(high - low, width, start - low), preferred_element_type=jnp.float32
        )
        level = total * inverse_ref[:, start : start + width] + norm_floor
        values = x_ref[w, :, start : start + width].astype(jnp.float32)
        normed_ref[:, start : start + width] = (values / level).astype(jnp.bfloat16)
    spectrum = jnp.dot(normed_ref[...], basis_ref[...], preferred_element_type=jnp.float32)
    square = spectrum * spectrum
    amplitude = jnp.sqrt(square + pltpu.roll(square, F, 1))
    bins = lax.broadcasted_iota(jnp.int32, (1, 2 * F), 1) % F
    first, last = bins == 0, bins == F - 1
    below = jnp.where(first, 0.0, pltpu.roll(amplitude, 1, 1))
    above = jnp.where(last, 0.0, pltpu.roll(amplitude, 2 * F - 1, 1))
    share = jnp.where(first | last, 1.0 / 2.0, 1.0 / 3.0)
    smooth = (below + amplitude + above) * share
    mean = jnp.sum(amplitude, axis=1, keepdims=True) * (0.5 / F)
    level = jnp.maximum(smooth, water_level * (mean + norm_floor))
    white = (spectrum * (taper_ref[...] / level)).astype(jnp.bfloat16)
    floor = lax.broadcasted_iota(jnp.int32, (rows, rows), 0) * src_count
    channel = channel_ref[...]
    pick = (channel >= floor) & (channel < floor + src_count)
    pick = pick.astype(jnp.float32).astype(jnp.bfloat16)
    ordered = jnp.dot(pick, white, preferred_element_type=jnp.float32).astype(jnp.bfloat16)
    return ordered.reshape(src_count, rows // src_count, 2 * F)


def spread_kernel(
    src_count, rcv_count, x_ref, channel_ref, taper_ref, inverse_ref, basis_ref, live_ref,
    block_ref, near_ref, rest_ref,
    normed_ref, ordered_ref, arrived_ref, own_ref,
    swap_send, swap_recv, block_send, block_recv, pass_send, near_send, near_recv, local_sem,
):
    src, rcv = lax.axis_index("src"), lax.axis_index("rcv")
    windows = x_ref.shape[0]
    half = own_ref.shape[3]
    pairs = rcv_count // 2
    row, core = rcv // 2, rcv % 2
    mate = rcv + 1 - 2 * core

    def slot(receiver, holder):
        return (receiver + rcv_count - holder) % rcv_count

    def signal(place):
        pl.semaphore_signal(barrier, inc=1, device_id=place, device_id_type=pl.DeviceIdType.MESH)

    def push(source, target, send_sem, recv_sem, place):
        return pltpu.make_async_remote_copy(
            src_ref=source,
            dst_ref=target,
            send_sem=send_sem,
            recv_sem=recv_sem,
            device_id=place,
            device_id_type=pl.DeviceIdType.MESH,
        )

    barrier = pltpu.get_barrier_semaphore()
    for k in range(1, src_count):
        signal(((src + k) % src_count, rcv))
    for k in range(1, rcv_count):
        signal((src, (rcv + k) % rcv_count))
    takes = (rcv >= 1) & (src + rcv < src_count)

    @pl.when(takes)
    def _():
        for k in range(rcv_count):
            signal((src + rcv, k))

    pl.semaphore_wait(
        barrier, src_count - 1 + rcv_count - 1 + jnp.minimum(src, rcv_count - 1)
    )

    def swap(w, k):
        target = (src + k) % src_count
        return push(
            ordered_ref.at[w, target],
            arrived_ref.at[w, src],
            swap_send.at[w, k],
            swap_recv.at[w, src],
            (target, rcv),
        )

    def swapped(w, k):
        source = (src + k) % src_count
        return push(
            ordered_ref.at[w, source],
            arrived_ref.at[w, source],
            swap_send.at[w, k],
            swap_recv.at[w, source],
            (source, rcv),
        )

    def share(w, k):
        to = mate if k == 0 else ((row + k) % pairs) * 2 + core
        place = slot(to, rcv)
        return push(
            own_ref.at[w], block_ref.at[place, w], block_send.at[w, k], block_recv.at[w, place], (src, to)
        )

    def shared(w, holder):
        place = slot(rcv, holder)
        return push(
            own_ref.at[w], block_ref.at[place, w], block_send.at[w, 0], block_recv.at[w, place], (src, mate)
        )

    def hand_on(w, k):
        holder = ((row + k) % pairs) * 2 + core
        place = slot(mate, holder)
        return push(
            block_ref.at[slot(rcv, holder), w],
            block_ref.at[place, w],
            pass_send.at[w, k],
            block_recv.at[w, place],
            (src, mate),
        )

    def near(w, to):
        place = slot(to, rcv)
        return push(
            own_ref.at[w, 0],
            near_ref.at[place, w],
            near_send.at[w, to],
            near_recv.at[w, place],
            (src - to, to),
        )

    def keep(w):
        return pltpu.make_async_copy(own_ref.at[w], block_ref.at[0, w], local_sem.at[w])

    for w in range(windows):
        ordered_ref[w] = whiten_window(
            w, src_count, x_ref, channel_ref, taper_ref, inverse_ref, basis_ref, normed_ref
        )
        for k in range(1, src_count):
            swap(w, k).start()

    for w in range(windows):
        for k in range(src_count):
            source = (src + k) % src_count
            if k:
                swapped(w, k).wait_recv()
                value = arrived_ref[w, source]
            else:
                value = ordered_ref[w, source]
            value = value * live_ref[source]
            own_ref[w, 0, source] = value[:half]
            own_ref[w, 1, source] = value[half:]
            rest_ref[w, source] = value[half:]
        for k in range(pairs):
            share(w, (k + 1) % pairs).start()
        for to in range(1, rcv_count):
            pl.when(src >= to)(lambda w=w, to=to: near(w, to).start())
        keep(w).start()

    for w in range(windows):
        for k in range(1, pairs):
            shared(w, ((row + k) % pairs) * 2 + core).wait_recv()
            hand_on(w, k).start()

    for w in range(windows):
        for k in range(pairs):
            shared(w, ((row + k) % pairs) * 2 + 1 - core).wait_recv()

        @pl.when(takes)
        def _(w=w):
            for k in range(rcv_count):
                push(
                    own_ref.at[w, 0], near_ref.at[k, w], near_send.at[w, 0], near_recv.at[w, k], (src + rcv, k)
                ).wait_recv()

        for k in range(1, src_count):
            swap(w, k).wait_send()
        for k in range(pairs):
            share(w, k).wait_send()
            if k:
                hand_on(w, k).wait_send()
        for to in range(1, rcv_count):
            pl.when(src >= to)(lambda w=w, to=to: near(w, to).wait_send())
        keep(w).wait()


def spread(raw_samples, channel_of_row, live_channels, bin_taper, src_count, rcv_count):
    windows, rows, length = raw_samples.shape
    part = rows // src_count
    half = part // 2
    lanes = 2 * F
    live = live_channels.reshape(part, src_count).T.astype(jnp.bfloat16)
    live = jnp.broadcast_to(live[:, None, :, None], (src_count, 1, part, lanes)).reshape(
        src_count, part, lanes
    )
    vmem = pl.BlockSpec(memory_space=pltpu.VMEM)
    anywhere = pl.BlockSpec(memory_space=pl.ANY)
    dma = pltpu.SemaphoreType.DMA
    return pl.pallas_call(
        functools.partial(spread_kernel, src_count, rcv_count),
        out_shape=[
            jax.ShapeDtypeStruct((rcv_count, windows, 2, src_count, half, lanes), jnp.bfloat16),
            jax.ShapeDtypeStruct((rcv_count, windows, src_count, half, lanes), jnp.bfloat16),
            jax.ShapeDtypeStruct((windows, src_count, half, lanes), jnp.bfloat16),
        ],
        in_specs=[vmem] * 6,
        out_specs=[anywhere, anywhere, vmem],
        scratch_shapes=[
            pltpu.VMEM((rows, length), jnp.bfloat16),
            pltpu.VMEM((windows, src_count, part, lanes), jnp.bfloat16),
            pltpu.VMEM((windows, src_count, part, lanes), jnp.bfloat16),
            pltpu.VMEM((windows, 2, src_count, half, lanes), jnp.bfloat16),
            dma((windows, src_count)),
            dma((windows, src_count)),
            dma((windows, rcv_count // 2)),
            dma((windows, rcv_count)),
            dma((windows, rcv_count // 2)),
            dma((windows, rcv_count)),
            dma((windows, rcv_count)),
            dma((windows,)),
        ],
        compiler_params=pltpu.CompilerParams(
            collective_id=0, has_side_effects=True, vmem_limit_bytes=48 << 20
        ),
        name="spread",
    )(
        raw_samples,
        channel_of_row.reshape(1, rows),
        jnp.tile(bin_taper, 2).reshape(1, lanes),
        jnp.asarray(inverse_counts(length)),
        jnp.asarray(basis_table(length)),
        live,
    )


def correlate_kernel(pieces, half_index, scale, *refs):
    refs = list(refs)
    block_ref = refs.pop(0)
    rcv_refs = [refs.pop(0) for _ in range(pieces if half_index else 1)]
    reach_ref, straight_ref, swapped_ref = refs[:3]
    if half_index:
        left_ref, _, out_ref = refs[3:6]
    else:
        out_ref, left_ref = refs[3:5]
    rcv_ref, turned_ref, even_ref, odd_ref = refs[-4:]
    step = pl.program_id(0)
    local, halves, src_count, half, lanes = block_ref.shape[1:]
    windows = pieces * local
    count = src_count * half
    rows = halves * count
    columns = CHUNK * LAGS
    src, rcv = lax.axis_index("src"), lax.axis_index("rcv")

    def rotate(first, target):
        straight = straight_ref[...][None]
        swapped = swapped_ref[...][None]
        for w in range(windows):
            plain = rcv_ref[pl.ds(first, CHUNK), w * lanes : (w + 1) * lanes]
            turned = turned_ref[pl.ds(first, CHUNK), w * lanes : (w + 1) * lanes]
            value = plain[:, None, :] * straight + turned[:, None, :] * swapped
            target[:, w * lanes : (w + 1) * lanes] = value.reshape(columns, lanes).astype(
                jnp.bfloat16
            )

    @pl.when(step == 0)
    def _():
        natural = lax.broadcasted_iota(jnp.int32, (count, count), 0)
        held = lax.broadcasted_iota(jnp.int32, (count, count), 1)
        pick = natural == (held % half) * src_count + held // half
        pick = pick.astype(jnp.float32).astype(jnp.bfloat16)
        for d in range(pieces):
            span = slice(d * local * lanes, (d + 1) * local * lanes)
            own = [
                jnp.concatenate(
                    [block_ref[d, n, h].reshape(count, lanes) for n in range(local)], axis=1
                )
                for h in range(halves)
            ]
            if not half_index:
                for h in range(halves):
                    left_ref[h * count : (h + 1) * count, span] = jnp.dot(
                        pick, own[h], preferred_element_type=jnp.float32
                    ).astype(jnp.bfloat16)
            source = rcv_refs[d] if half_index else rcv_refs[0].at[d]
            other = jnp.concatenate(
                [source[n].reshape(count, lanes) for n in range(local)], axis=1
            )
            block = jnp.where(rcv == 0, own[half_index], other)
            value = jnp.dot(pick, block, preferred_element_type=jnp.float32)
            rcv_ref[:, span] = value
            for n in range(local):
                at = (d * local + n) * lanes
                turned_ref[:, at : at + lanes] = pltpu.roll(
                    value[:, n * lanes : (n + 1) * lanes], F, 1
                )
        rotate(0, even_ref)

    low = (lax.broadcasted_iota(jnp.int32, (rows, 1), 0) - rcv * rows) * LAGS
    high = low + reach_ref[...] * LAGS + (LAGS - 1)
    high = jnp.where(src + rcv < src_count, high, -1)

    def multiply(source, turn):
        total = lax.dot_general(
            left_ref[...], source[...], (((1,), (1,)), ((), ())), preferred_element_type=jnp.float32
        )
        column = lax.broadcasted_iota(jnp.int32, (1, columns), 1)
        column = column + (2 * step + turn) * columns + half_index * count * LAGS
        keep = (column >= low) & (column <= high)
        out_ref[:, turn * columns : (turn + 1) * columns] = jnp.where(
            keep, total * scale, 0.0
        ).astype(jnp.bfloat16)

    multiply(even_ref, 0)
    rotate((2 * step + 1) * CHUNK, odd_ref)
    multiply(odd_ref, 1)
    rotate(jnp.minimum(2 * step + 2, count // CHUNK - 1) * CHUNK, even_ref)


def correlate(block, receivers, band_reach, length, earlier=None):
    half_index = int(earlier is not None)
    pieces, local, halves, src_count, half, lanes = block.shape
    count = src_count * half
    rows = halves * count
    windows = pieces * local
    depth = windows * lanes
    columns = CHUNK * LAGS
    steps = count // (2 * CHUNK)
    straight, swapped = lag_tables(length)
    whole = lambda *shape: pl.BlockSpec(shape, lambda g: (0,) * len(shape))
    operands = [
        block, *receivers, band_reach.reshape(rows, 1), jnp.asarray(straight), jnp.asarray(swapped)
    ]
    in_specs = [whole(*operand.shape) for operand in operands]
    out_shape = [jax.ShapeDtypeStruct((rows, rows * LAGS), jnp.bfloat16)]
    out_specs = [pl.BlockSpec((rows, 2 * columns), lambda g: (0, g + half_index * steps))]
    aliases = {}
    if half_index:
        operands += [earlier[1], earlier[0]]
        in_specs += [whole(rows, depth), pl.BlockSpec(memory_space=pl.ANY)]
        aliases = {len(operands) - 1: 0}
    else:
        out_shape.append(jax.ShapeDtypeStruct((rows, depth), jnp.bfloat16))
        out_specs.append(whole(rows, depth))
    return pl.pallas_call(
        functools.partial(correlate_kernel, pieces, half_index, 1.0 / math.sqrt(windows)),
        grid=(steps,),
        out_shape=out_shape,
        in_specs=in_specs,
        out_specs=out_specs,
        scratch_shapes=[
            pltpu.VMEM((count, depth), jnp.float32),
            pltpu.VMEM((count, depth), jnp.float32),
            pltpu.VMEM((columns, depth), jnp.bfloat16),
            pltpu.VMEM((columns, depth), jnp.bfloat16),
        ],
        input_output_aliases=aliases,
        cost_estimate=pl.CostEstimate(
            flops=2 * rows * depth * count * LAGS,
            bytes_accessed=2 * rows * count * LAGS,
            transcendentals=0,
        ),
        compiler_params=pltpu.CompilerParams(vmem_limit_bytes=56 << 20),
        name="correlate",
    )(*operands)


def body(raw_samples, channel_of_row, live_channels, band_reach, bin_taper):
    src_count = lax.axis_size("src")
    rcv_count = lax.axis_size("rcv")
    length = raw_samples.shape[2]
    block, near, rest = spread(
        raw_samples, channel_of_row, live_channels, bin_taper, src_count, rcv_count
    )
    far = []
    for d in range(rcv_count):
        route = []
        for s in range(src_count):
            for r in range(rcv_count):
                to = (r + d) % rcv_count
                if to and s >= to:
                    route.append((s * rcv_count + r, (s - to) * rcv_count + to))
        far.append(lax.ppermute(rest, ("src", "rcv"), route))
    earlier = correlate(block, [near], band_reach, length)
    return correlate(block, far, band_reach, length, earlier)[0]


def solution(mesh):
    return jax.shard_map(
        body,
        mesh=mesh,
        in_specs=(P("rcv", "src", None), P("src"), P("src"), P("src"), P()),
        out_specs=P("src", "rcv"),
        check_vma=False,
    )
```

time: 119 us -> 100 us (0.84)
  the two profiles are of different devices: /device:TPU:6 before, /device:TPU:19 now
where the time goes in v2:
time: 100 us
  Pallas kernels  72.6 us (73%)
  starting transfers between devices  17.6 us (18%)
  local copies, waits for them, and re-layouts  9.04 us (9%)
    pallas_call x2, Pallas kernels, correlate(): pl.pallas_call(functools.partial(correlate_kernel, pieces, half_index, 1....  46.6 us
    pallas_call x1, Pallas kernels, spread(): pl.pallas_call(functools.partial(spread_kernel, src_count, rcv_count), ou...  25.9 us
    ppermute x4, starting transfers between devices, body(): far.append(lax.ppermute(rest, ('src', 'rcv'), route))  17.6 us
    unnamed x22, local copies, waits for them, and re-layouts  7.13 us
  transfers between devices with their start and end apart: 4, of which 0 were waited for; matrix products, arithmetic and copies ran while one was open for 1% of the time, Pallas kernels for 23%

profile of v2, /device:TPU:19, one launch (start us, length us, event | category | flops | bytes accessed | tf_op | source)
XLA Modules:
  0.0 100.0 jit_solution(12486532705378183359)
XLA Ops:
  0.0 0.0 copy-start.6
  0.0 0.7 convert_element_type.9
  0.7 0.7 tile.2
  1.4 0.1 reshape_tile.3.taper_ref
  1.4 0.1 convert_element_type.10
  1.5 0.1 copy.13
  1.6 0.2 reshape.17.live_ref
  1.8 0.0 copy-start
  1.8 1.9 %copy-done = bf16[3,512,1024]{2,1,0:T(8,128)(2,1)S(1)} copy-done((bf16[3,512,1024]{2,1,0:T(8,128)(2,1)S(1)}, bf16[3,512,1024]{2,1,0:T(8,128)(2,1)}, u32[]{:S(2)}) %copy-start) | copy-done | bytes 3145752
  3.7 0.0 copy-start.1
  3.7 0.9 copy-done.1
  4.6 0.0 copy-start.2
  4.6 0.7 copy-done.2
  5.3 0.0 copy-start.3
  5.3 0.7 copy-done.3
  6.0 25.9 %spread.1 = (bf16[4,3,2,8,32,128]{5,4,3,2,1,0:T(8,128)(2,1)S(1)}, bf16[4,3,8,32,128]{4,3,2,1,0:T(8,128)(2,1)S(1)}, bf16[3,8,32,128]{3,2,1,0:T(8,128)(2,1)S(1)}) custom-call(bf16[3,512,1024]{2,1,0:T(8,128)(2,1)S(1)} %copy-done, s32[1,512]{1,0:T(1,128)S(1)} %bitcast.3, f32[1,128]{1,0:T(1,128)S(1)} %reshape_tile.3.taper_ref, f32[1,1024]{1,0:T(1,128)S(1)} %copy-done.2, ...), custom_call_target="tpu_custom_call" | custom-call | tf_op jit(solution)/shard_map/spread/pallas_call | solution.py:257
  31.9 0.0 copy-start.4
  31.9 1.2 %copy-done.4 = bf16[4,3,2,8,32,128]{5,4,3,2,1,0:T(8,128)(2,1)} copy-done((bf16[4,3,2,8,32,128]{5,4,3,2,1,0:T(8,128)(2,1)}, bf16[4,3,2,8,32,128]{5,4,3,2,1,0:T(8,128)(2,1)S(1)}, u32[]{:S(2)}) %copy-start.4) | copy-done | bytes 1572888
  33.1 0.0 copy-start.5
  33.1 0.9 copy-done.5
  34.0 1.3 %collective-permute-start.3 = (bf16[3,8,32,128]{3,2,1,0:T(8,128)(2,1)S(1)}, bf16[3,8,32,128]{3,2,1,0:T(8,128)(2,1)S(1)}, u32[]{:S(2)}, u32[]{:S(2)}) collective-permute-start(bf16[3,8,32,128]{3,2,1,0:T(8,128)(2,1)S(1)} %get-tuple-element.11), channel_id=1, source_target_pairs={{6,1},{10,5},{11,2},{12,3},{14,9},{15,6},{16,7},{18,13},{19,10},{2... | collective-permute-start | bytes 589832 | tf_op jit(solution)/shard_map/ppermute | solution.py:440
  35.3 10.2 %collective-permute-start.2 = (bf16[3,8,32,128]{3,2,1,0:T(8,128)(2,1)S(1)}, bf16[3,8,32,128]{3,2,1,0:T(8,128)(2,1)S(1)}, u32[]{:S(2)}, u32[]{:S(2)}) collective-permute-start(bf16[3,8,32,128]{3,2,1,0:T(8,128)(2,1)S(1)} %get-tuple-element.11), channel_id=1, source_target_pairs={{7,1},{8,2},{11,5},{12,6},{13,3},{15,9},{16,10},{17,7},{19,13},{20... | collective-permute-start | bytes 589832 | tf_op jit(solution)/shard_map/ppermute | solution.py:440
  45.5 1.9 %collective-permute-start.1 = (bf16[3,8,32,128]{3,2,1,0:T(8,128)(2,1)S(1)}, bf16[3,8,32,128]{3,2,1,0:T(8,128)(2,1)S(1)}, u32[]{:S(2)}, u32[]{:S(2)}) collective-permute-start(bf16[3,8,32,128]{3,2,1,0:T(8,128)(2,1)S(1)} %get-tuple-element.11), channel_id=1, source_target_pairs={{4,1},{8,5},{9,2},{12,9},{13,6},{14,3},{16,13},{17,10},{18,7},{20,... | collective-permute-start | bytes 589832 | tf_op jit(solution)/shard_map/ppermute | solution.py:440
  47.5 4.1 %collective-permute-start = (bf16[3,8,32,128]{3,2,1,0:T(8,128)(2,1)S(1)}, bf16[3,8,32,128]{3,2,1,0:T(8,128)(2,1)S(1)}, u32[]{:S(2)}, u32[]{:S(2)}) collective-permute-start(bf16[3,8,32,128]{3,2,1,0:T(8,128)(2,1)S(1)} %get-tuple-element.11), channel_id=1, source_target_pairs={{5,1},{9,5},{10,2},{13,9},{14,6},{15,3},{17,13},{18,10},{19,7},{21... | collective-permute-start | bytes 589832 | tf_op jit(solution)/shard_map/ppermute | solution.py:440
  51.6 0.0 copy-done.6
  51.6 0.8 copy.15.refs_2_.refs_5_
  52.5 22.7 %correlate.2 = (bf16[512,16384]{1,0:T(8,128)(2,1)}, bf16[512,1536]{1,0:T(8,128)(2,1)}) custom-call(bf16[4,3,2,8,32,128]{5,4,3,2,1,0:T(8,128)(2,1)} %copy-done.4, bf16[4,3,8,32,128]{4,3,2,1,0:T(8,128)(2,1)} %copy-done.5, s32[512,1]{1,0:T(8,128)} %copy.15.refs_2_.refs_5_, f32[32,128]{1,0:T(8,128)} %constant.10.clone.refs_3_.refs_6_, ...), custom_call_target="tpu_custom_call" | custom-call | flops 12884901888 | bytes 8388608 | tf_op jit(solution)/shard_map/correlate/pallas_call | solution.py:402
  75.1 0.0 collective-permute-done.3.refs_4_
  75.2 0.0 copy-start.7
  75.2 0.0 collective-permute-done.2.refs_3_
  75.2 0.0 copy-start.8
  75.2 0.0 collective-permute-done.1.refs_2_
  75.2 0.0 copy-start.9
  75.2 0.0 collective-permute-done.refs_1_
  75.2 0.0 copy-start.10
  75.2 0.6 copy-done.7
  75.8 0.1 copy-done.8
  75.9 0.1 copy-done.9
  76.0 0.1 copy-done.10
  76.1 23.9 %correlate.3 = bf16[512,16384]{1,0:T(8,128)(2,1)} custom-call(bf16[4,3,2,8,32,128]{5,4,3,2,1,0:T(8,128)(2,1)} %copy-done.4, bf16[3,8,32,128]{3,2,1,0:T(8,128)(2,1)} %copy-done.10, bf16[3,8,32,128]{3,2,1,0:T(8,128)(2,1)} %copy-done.9, bf16[3,8,32,128]{3,2,1,0:T(8,128)(2,1)} %copy-done.8, ...), custom_call_target="tpu_custom_call", output_to_operand_aliasing={{}: (9, {})} | custom-call | flops 12884901888 | bytes 8388608 | tf_op jit(solution)/shard_map/correlate/pallas_call | solution.py:402
Async XLA Ops:
  0.0 51.6 %copy-start.6 = (s32[512]{0:T(512)S(1)}, s32[512]{0:T(512)}, u32[]{:S(2)}) copy-start(s32[512]{0:T(512)} %param.14) | copy-start | bytes 6148
  1.8 1.9 %copy-start = (bf16[3,512,1024]{2,1,0:T(8,128)(2,1)S(1)}, bf16[3,512,1024]{2,1,0:T(8,128)(2,1)}, u32[]{:S(2)}) copy-start(bf16[3,512,1024]{2,1,0:T(8,128)(2,1)} %x_ref.1) | copy-start | bytes 9437188
  3.7 0.9 copy-start.1
  4.6 0.7 copy-start.2
  5.3 0.7 copy-start.3
  31.9 1.2 %copy-start.4 = (bf16[4,3,2,8,32,128]{5,4,3,2,1,0:T(8,128)(2,1)}, bf16[4,3,2,8,32,128]{5,4,3,2,1,0:T(8,128)(2,1)S(1)}, u32[]{:S(2)}) copy-start(bf16[4,3,2,8,32,128]{5,4,3,2,1,0:T(8,128)(2,1)S(1)} %get-tuple-element.10.refs_0_) | copy-start | bytes 4718596
  33.1 0.9 copy-start.5
  34.0 41.1 %collective-permute-start.3 = (bf16[3,8,32,128]{3,2,1,0:T(8,128)(2,1)S(1)}, bf16[3,8,32,128]{3,2,1,0:T(8,128)(2,1)S(1)}, u32[]{:S(2)}, u32[]{:S(2)}) collective-permute-start(bf16[3,8,32,128]{3,2,1,0:T(8,128)(2,1)S(1)} %get-tuple-element.11), channel_id=1, source_target_pairs={{6,1},{10,5},{11,2},{12,3},{14,9},{15,6},{16,7},{18,13},{19,10},{2... | collective-permute-start | bytes 589832 | tf_op jit(solution)/shard_map/ppermute | solution.py:440
  35.3 39.9 %collective-permute-start.2 = (bf16[3,8,32,128]{3,2,1,0:T(8,128)(2,1)S(1)}, bf16[3,8,32,128]{3,2,1,0:T(8,128)(2,1)S(1)}, u32[]{:S(2)}, u32[]{:S(2)}) collective-permute-start(bf16[3,8,32,128]{3,2,1,0:T(8,128)(2,1)S(1)} %get-tuple-element.11), channel_id=1, source_target_pairs={{7,1},{8,2},{11,5},{12,6},{13,3},{15,9},{16,10},{17,7},{19,13},{20... | collective-permute-start | bytes 589832 | tf_op jit(solution)/shard_map/ppermute | solution.py:440
  45.5 29.6 %collective-permute-start.1 = (bf16[3,8,32,128]{3,2,1,0:T(8,128)(2,1)S(1)}, bf16[3,8,32,128]{3,2,1,0:T(8,128)(2,1)S(1)}, u32[]{:S(2)}, u32[]{:S(2)}) collective-permute-start(bf16[3,8,32,128]{3,2,1,0:T(8,128)(2,1)S(1)} %get-tuple-element.11), channel_id=1, source_target_pairs={{4,1},{8,5},{9,2},{12,9},{13,6},{14,3},{16,13},{17,10},{18,7},{20,... | collective-permute-start | bytes 589832 | tf_op jit(solution)/shard_map/ppermute | solution.py:440
  47.5 27.7 %collective-permute-start = (bf16[3,8,32,128]{3,2,1,0:T(8,128)(2,1)S(1)}, bf16[3,8,32,128]{3,2,1,0:T(8,128)(2,1)S(1)}, u32[]{:S(2)}, u32[]{:S(2)}) collective-permute-start(bf16[3,8,32,128]{3,2,1,0:T(8,128)(2,1)S(1)} %get-tuple-element.11), channel_id=1, source_target_pairs={{5,1},{9,5},{10,2},{13,9},{14,6},{15,3},{17,13},{18,10},{19,7},{21... | collective-permute-start | bytes 589832 | tf_op jit(solution)/shard_map/ppermute | solution.py:440
  75.2 0.7 copy-start.7
  75.2 0.8 copy-start.8
  75.2 0.8 copy-start.9
  75.2 0.9 copy-start.10

commit v3 on v2

v3 whole, which is shorter than its diff:
```python
import functools
import math

import jax
import jax.numpy as jnp
import ml_dtypes
import numpy as np
from jax import lax
from jax.experimental import pallas as pl
from jax.experimental.pallas import tpu as pltpu
from jax.sharding import PartitionSpec as P

F = 64
K0 = 32
HW = 64
LAGS = 32
CHUNK = 16

norm_floor = 1e-05
water_level = 0.3


def basis_table(length):
    sample_index = np.arange(length)
    bin_index = np.arange(F) + K0
    phase = np.mod(sample_index[:, None] * bin_index[None, :], length)
    angle = phase * (2.0 * math.pi / length)
    table = np.concatenate([np.cos(angle), -np.sin(angle)], axis=1)
    return table.astype(np.float32).astype(ml_dtypes.bfloat16)


def lag_tables(length):
    bin_index = np.arange(F) + K0
    lag_index = np.arange(LAGS) - LAGS // 2
    phase = np.mod(lag_index[:, None] * bin_index[None, :], length)
    angle = phase * (2.0 * math.pi / length)
    scale = 1.0 / math.sqrt(F)
    cosine = (np.cos(angle) * scale).astype(np.float32).astype(ml_dtypes.bfloat16)
    sine = (np.sin(angle) * scale).astype(np.float32).astype(ml_dtypes.bfloat16)
    straight = np.concatenate([cosine, cosine], axis=1).astype(np.float32)
    swapped = np.concatenate([-sine, sine], axis=1).astype(np.float32)
    return straight, swapped


def inverse_counts(start, width, length):
    position = lax.broadcasted_iota(jnp.int32, (1, width), 1) + start
    upper = jnp.minimum(position + HW, length - 1)
    lower = jnp.maximum(position - HW, 0)
    return 1.0 / (upper - lower + 1).astype(jnp.float32)


def band(rows, columns, shift):
    row = lax.broadcasted_iota(jnp.int32, (rows, columns), 0)
    column = lax.broadcasted_iota(jnp.int32, (rows, columns), 1)
    return (jnp.abs(row - column - shift) <= HW).astype(jnp.float32).astype(jnp.bfloat16)


def whiten_window(w, src_count, x_ref, channel_ref, taper_ref, basis_ref, normed_ref):
    rows, length = x_ref.shape[1:]
    width = 256
    for start in range(0, length, width):
        low = max(start - 128, 0)
        high = min(start + width + 128, length)
        magnitude = jnp.abs(x_ref[w, :, low:high])
        total = jnp.dot(
            magnitude, band(high - low, width, start - low), preferred_element_type=jnp.float32
        )
        level = total * inverse_counts(start, width, length) + norm_floor
        values = x_ref[w, :, start : start + width].astype(jnp.float32)
        normed_ref[:, start : start + width] = (values / level).astype(jnp.bfloat16)
    spectrum = jnp.dot(normed_ref[...], basis_ref[...], preferred_element_type=jnp.float32)
    square = spectrum * spectrum
    amplitude = jnp.sqrt(square + pltpu.roll(square, F, 1))
    bins = lax.broadcasted_iota(jnp.int32, (1, 2 * F), 1) % F
    first, last = bins == 0, bins == F - 1
    below = jnp.where(first, 0.0, pltpu.roll(amplitude, 1, 1))
    above = jnp.where(last, 0.0, pltpu.roll(amplitude, 2 * F - 1, 1))
    share = jnp.where(first | last, 1.0 / 2.0, 1.0 / 3.0)
    smooth = (below + amplitude + above) * share
    mean = jnp.sum(amplitude, axis=1, keepdims=True) * (0.5 / F)
    level = jnp.maximum(smooth, water_level * (mean + norm_floor))
    taper = jnp.concatenate([taper_ref[...], taper_ref[...]], axis=1)
    white = (spectrum * (taper / level)).astype(jnp.bfloat16)
    floor = lax.broadcasted_iota(jnp.int32, (rows, rows), 0) * src_count
    channel = channel_ref[...]
    pick = (channel >= floor) & (channel < floor + src_count)
    pick = pick.astype(jnp.float32).astype(jnp.bfloat16)
    ordered = jnp.dot(pick, white, preferred_element_type=jnp.float32).astype(jnp.bfloat16)
    return ordered.reshape(src_count, rows // src_count, 2 * F)


def spread_kernel(
    src_count, rcv_count, raw_ref, channel_hbm, taper_hbm, basis_hbm, live_hbm,
    first_ref, second_ref, near_ref,
    x_ref, channel_ref, taper_ref, basis_ref, live_ref, mask_ref, normed_ref, ordered_ref, arrived_ref, own_ref,
    swap_send, swap_recv, block_send, block_recv, pass_send, near_send, near_recv, local_sem,
    load_sem, table_sem,
):
    src, rcv = lax.axis_index("src"), lax.axis_index("rcv")
    windows, rows = x_ref.shape[:2]
    half = own_ref.shape[2]
    block_refs = (first_ref, second_ref)

    def load(w):
        return pltpu.make_async_copy(raw_ref.at[w], x_ref.at[w], load_sem.at[w])

    tables = [
        pltpu.make_async_copy(source, target, table_sem.at[n])
        for n, (source, target) in enumerate(
            [
                (live_hbm, live_ref),
                (channel_hbm, channel_ref),
                (taper_hbm, taper_ref),
                (basis_hbm, basis_ref),
            ]
        )
    ]
    for table in tables:
        table.start()
    load(0).start()
    for w in range(1, windows):
        load(w).start()
    pairs = rcv_count // 2
    row, core = rcv // 2, rcv % 2
    mate = rcv + 1 - 2 * core

    def slot(receiver, holder):
        return (receiver + rcv_count - holder) % rcv_count

    def signal(place):
        pl.semaphore_signal(barrier, inc=1, device_id=place, device_id_type=pl.DeviceIdType.MESH)

    def push(source, target, send_sem, recv_sem, place):
        return pltpu.make_async_remote_copy(
            src_ref=source,
            dst_ref=target,
            send_sem=send_sem,
            recv_sem=recv_sem,
            device_id=place,
            device_id_type=pl.DeviceIdType.MESH,
        )

    barrier = pltpu.get_barrier_semaphore()
    for k in range(1, src_count):
        signal(((src + k) % src_count, rcv))
    for k in range(1, rcv_count):
        signal((src, (rcv + k) % rcv_count))
    takes = (rcv >= 1) & (src + rcv < src_count)

    @pl.when(takes)
    def _():
        for k in range(rcv_count):
            signal((src + rcv, k))

    def swap(w, k):
        target = (src + k) % src_count
        return push(
            ordered_ref.at[w, target],
            arrived_ref.at[w, src],
            swap_send.at[w, k],
            swap_recv.at[w, src],
            (target, rcv),
        )

    def swapped(w, k):
        source = (src + k) % src_count
        return push(
            ordered_ref.at[w, source],
            arrived_ref.at[w, source],
            swap_send.at[w, k],
            swap_recv.at[w, source],
            (source, rcv),
        )

    def share(w, h, k):
        to = mate if k == 0 else ((row + k) % pairs) * 2 + core
        place = slot(to, rcv)
        return push(
            own_ref.at[2 * w + h],
            block_refs[h].at[place, w],
            block_send.at[2 * w + h, k],
            block_recv.at[2 * w + h, place],
            (src, to),
        )

    def shared(w, h, holder):
        place = slot(rcv, holder)
        return push(
            own_ref.at[2 * w + h],
            block_refs[h].at[place, w],
            block_send.at[2 * w + h, 0],
            block_recv.at[2 * w + h, place],
            (src, mate),
        )

    def hand_on(w, h, k):
        holder = ((row + k) % pairs) * 2 + core
        place = slot(mate, holder)
        return push(
            block_refs[h].at[slot(rcv, holder), w],
            block_refs[h].at[place, w],
            pass_send.at[2 * w + h, k],
            block_recv.at[2 * w + h, place],
            (src, mate),
        )

    def near(w, to):
        place = slot(to, rcv)
        return push(
            own_ref.at[2 * w],
            near_ref.at[place, w],
            near_send.at[w, to],
            near_recv.at[w, place],
            (src - to, to),
        )

    def keep(w, h):
        return pltpu.make_async_copy(
            own_ref.at[2 * w + h], block_refs[h].at[0, w], local_sem.at[2 * w + h]
        )

    for table in tables:
        table.wait()
    held = lax.broadcasted_iota(jnp.int32, (rows, rows), 0)
    natural = lax.broadcasted_iota(jnp.int32, (rows, rows), 1)
    part = 2 * half
    pick = natural == (held % part) * src_count + held // part
    pick = jnp.where(pick, live_ref[...].astype(jnp.float32), 0.0).astype(jnp.bfloat16)
    ones = jnp.ones((rows, 2 * F), jnp.bfloat16)
    mask = jnp.dot(pick, ones, preferred_element_type=jnp.float32).astype(jnp.bfloat16)
    mask_ref[...] = mask.reshape(src_count, part, 2 * F)
    for w in range(windows):
        load(w).wait()
        ordered_ref[w] = whiten_window(
            w, src_count, x_ref, channel_ref, taper_ref, basis_ref, normed_ref
        )
        if w == 0:
            pl.semaphore_wait(
                barrier, src_count - 1 + rcv_count - 1 + jnp.minimum(src, rcv_count - 1)
            )
        for k in range(1, src_count):
            swap(w, k).start()

    for w in range(windows):
        for k in range(src_count):
            source = (src + k) % src_count
            if k:
                swapped(w, k).wait_recv()
                value = arrived_ref[w, source]
            else:
                value = ordered_ref[w, source]
            value = value * mask_ref[source]
            own_ref[2 * w, source] = value[:half]
            own_ref[2 * w + 1, source] = value[half:]
        for h in range(2):
            for k in range(pairs):
                share(w, h, (k + 1) % pairs).start()
            if h == 0:
                for to in range(1, rcv_count):
                    pl.when(src >= to)(lambda w=w, to=to: near(w, to).start())
            keep(w, h).start()

    for w in range(windows):
        for h in range(2):
            for k in range(1, pairs):
                shared(w, h, ((row + k) % pairs) * 2 + core).wait_recv()
                hand_on(w, h, k).start()

    for w in range(windows):
        for h in range(2):
            for k in range(pairs):
                shared(w, h, ((row + k) % pairs) * 2 + 1 - core).wait_recv()

        @pl.when(takes)
        def _(w=w):
            for k in range(rcv_count):
                push(
                    own_ref.at[2 * w], near_ref.at[k, w], near_send.at[w, 0], near_recv.at[w, k], (src + rcv, k)
                ).wait_recv()

        for k in range(1, src_count):
            swap(w, k).wait_send()
        for h in range(2):
            for k in range(pairs):
                share(w, h, k).wait_send()
                if k:
                    hand_on(w, h, k).wait_send()
            keep(w, h).wait()
        for to in range(1, rcv_count):
            pl.when(src >= to)(lambda w=w, to=to: near(w, to).wait_send())


def spread(raw_samples, channel_of_row, live_channels, bin_taper, src_count, rcv_count):
    windows, rows, length = raw_samples.shape
    part = rows // src_count
    half = part // 2
    lanes = 2 * F
    hbm = pl.BlockSpec(memory_space=pltpu.HBM)
    anywhere = pl.BlockSpec(memory_space=pl.ANY)
    dma = pltpu.SemaphoreType.DMA
    gathered = jax.ShapeDtypeStruct((rcv_count, windows, src_count, half, lanes), jnp.bfloat16)
    return pl.pallas_call(
        functools.partial(spread_kernel, src_count, rcv_count),
        out_shape=[gathered] * 3,
        in_specs=[hbm] * 5,
        out_specs=[anywhere] * 3,
        scratch_shapes=[
            pltpu.VMEM((windows, rows, length), jnp.bfloat16),
            pltpu.VMEM((1, rows), jnp.int32),
            pltpu.VMEM((1, F), jnp.float32),
            pltpu.VMEM((length, lanes), jnp.bfloat16),
            pltpu.VMEM((1, rows), jnp.int32),
            pltpu.VMEM((src_count, part, lanes), jnp.bfloat16),
            pltpu.VMEM((rows, length), jnp.bfloat16),
            pltpu.VMEM((windows, src_count, part, lanes), jnp.bfloat16),
            pltpu.VMEM((windows, src_count, part, lanes), jnp.bfloat16),
            pltpu.VMEM((2 * windows, src_count, half, lanes), jnp.bfloat16),
            dma((windows, src_count)),
            dma((windows, src_count)),
            dma((2 * windows, rcv_count // 2)),
            dma((2 * windows, rcv_count)),
            dma((2 * windows, rcv_count // 2)),
            dma((windows, rcv_count)),
            dma((windows, rcv_count)),
            dma((2 * windows,)),
            dma((windows,)),
            dma((4,)),
        ],
        compiler_params=pltpu.CompilerParams(
            collective_id=0, has_side_effects=True, vmem_limit_bytes=64 << 20
        ),
        name="spread",
    )(
        raw_samples,
        channel_of_row.reshape(1, rows),
        bin_taper.reshape(1, F),
        jnp.asarray(basis_table(length)),
        live_channels.reshape(1, rows),
    )


def correlate_kernel(pieces, half_index, scale, *refs):
    if half_index:
        own_refs = {1: refs[0]}
        source_ref, *small_refs, left_ref, _, out_ref = refs[1:8]
    else:
        own_refs = dict(enumerate(refs[:2]))
        source_ref, *small_refs, out_ref, left_ref = refs[2:8]
    reach_ref, straight_ref, swapped_ref, small_sem = refs[8:12]
    high_ref, rcv_ref, turned_ref, even_ref, odd_ref = refs[12:]
    step = pl.program_id(0)
    local, src_count, half, lanes = source_ref.shape[1:]
    halves = 2
    windows = pieces * local
    count = src_count * half
    rows = halves * count
    columns = CHUNK * LAGS
    src, rcv = lax.axis_index("src"), lax.axis_index("rcv")

    def rotate(first, target):
        straight = straight_ref[...][None]
        swapped = swapped_ref[...][None]
        for w in range(windows):
            plain = rcv_ref[pl.ds(first, CHUNK), w * lanes : (w + 1) * lanes]
            turned = turned_ref[pl.ds(first, CHUNK), w * lanes : (w + 1) * lanes]
            value = plain[:, None, :] * straight + turned[:, None, :] * swapped
            target[:, w * lanes : (w + 1) * lanes] = value.reshape(columns, lanes).astype(
                jnp.bfloat16
            )

    @pl.when(step == 0)
    def _():
        copies = [
            pltpu.make_async_copy(source, target, small_sem.at[n])
            for n, (source, target) in enumerate(
                zip(small_refs, (reach_ref, straight_ref, swapped_ref))
            )
        ]
        for copy in copies:
            copy.start()
        natural = lax.broadcasted_iota(jnp.int32, (count, count), 0)
        held = lax.broadcasted_iota(jnp.int32, (count, count), 1)
        pick = natural == (held % half) * src_count + held // half
        pick = pick.astype(jnp.float32).astype(jnp.bfloat16)
        for d in range(pieces):
            span = slice(d * local * lanes, (d + 1) * local * lanes)
            own = {
                h: jnp.concatenate([ref[d, n].reshape(count, lanes) for n in range(local)], axis=1)
                for h, ref in own_refs.items()
            }
            if not half_index:
                for h in range(halves):
                    left_ref[h * count : (h + 1) * count, span] = jnp.dot(
                        pick, own[h], preferred_element_type=jnp.float32
                    ).astype(jnp.bfloat16)
            other = jnp.concatenate(
                [source_ref[d, n].reshape(count, lanes) for n in range(local)], axis=1
            )
            block = jnp.where(rcv == 0, own[half_index], other)
            value = jnp.dot(pick, block, preferred_element_type=jnp.float32)
            rcv_ref[:, span] = value
            for n in range(local):
                at = (d * local + n) * lanes
                turned_ref[:, at : at + lanes] = pltpu.roll(
                    value[:, n * lanes : (n + 1) * lanes], F, 1
                )
        for copy in copies:
            copy.wait()
        rotate(0, even_ref)
        row = lax.broadcasted_iota(jnp.int32, (rows, rows), 0)
        column = lax.broadcasted_iota(jnp.int32, (rows, rows), 1)
        reach = jnp.where(row == column, reach_ref[...].astype(jnp.float32), 0.0)
        reach = jnp.sum(reach, axis=1, keepdims=True).astype(jnp.int32)
        first = (lax.broadcasted_iota(jnp.int32, (rows, 1), 0) - rcv * rows) * LAGS
        last = first + reach * LAGS + (LAGS - 1)
        high_ref[...] = jnp.where(src + rcv < src_count, last, -1)

    low = (lax.broadcasted_iota(jnp.int32, (rows, 1), 0) - rcv * rows) * LAGS
    high = high_ref[...]

    def multiply(source, turn):
        total = lax.dot_general(
            left_ref[...], source[...], (((1,), (1,)), ((), ())), preferred_element_type=jnp.float32
        )
        column = lax.broadcasted_iota(jnp.int32, (1, columns), 1)
        column = column + (2 * step + turn) * columns + half_index * count * LAGS
        keep = (column >= low) & (column <= high)
        out_ref[:, turn * columns : (turn + 1) * columns] = jnp.where(
            keep, total * scale, 0.0
        ).astype(jnp.bfloat16)

    rotate((2 * step + 1) * CHUNK, odd_ref)
    multiply(even_ref, 0)
    rotate(jnp.minimum(2 * step + 2, count // CHUNK - 1) * CHUNK, even_ref)
    multiply(odd_ref, 1)


def correlate(blocks, receivers, band_reach, length, earlier=None):
    half_index = int(earlier is not None)
    pieces, local, src_count, half, lanes = receivers.shape
    halves = 2
    count = src_count * half
    rows = halves * count
    windows = pieces * local
    depth = windows * lanes
    columns = CHUNK * LAGS
    steps = count // (2 * CHUNK)
    straight, swapped = lag_tables(length)
    whole = lambda *shape: pl.BlockSpec(shape, lambda g: (0,) * len(shape))
    operands = [
        *blocks, receivers, band_reach.reshape(1, rows), jnp.asarray(straight), jnp.asarray(swapped)
    ]
    in_specs = [whole(*operand.shape) for operand in operands]
    in_specs[-3:] = [pl.BlockSpec(memory_space=pltpu.HBM)] * 3
    out_shape = [jax.ShapeDtypeStruct((rows, rows * LAGS), jnp.bfloat16)]
    out_specs = [pl.BlockSpec((rows, 2 * columns), lambda g: (0, g + half_index * steps))]
    aliases = {}
    if half_index:
        operands += [earlier[1], earlier[0]]
        in_specs += [whole(rows, depth), pl.BlockSpec(memory_space=pl.ANY)]
        aliases = {len(operands) - 1: 0}
    else:
        out_shape.append(jax.ShapeDtypeStruct((rows, depth), jnp.bfloat16))
        out_specs.append(whole(rows, depth))
    return pl.pallas_call(
        functools.partial(correlate_kernel, pieces, half_index, 1.0 / math.sqrt(windows)),
        grid=(steps,),
        out_shape=out_shape,
        in_specs=in_specs,
        out_specs=out_specs,
        scratch_shapes=[
            pltpu.VMEM((1, rows), jnp.int32),
            pltpu.VMEM((LAGS, lanes), jnp.float32),
            pltpu.VMEM((LAGS, lanes), jnp.float32),
            pltpu.SemaphoreType.DMA((3,)),
            pltpu.VMEM((rows, 1), jnp.int32),
            pltpu.VMEM((count, depth), jnp.float32),
            pltpu.VMEM((count, depth), jnp.float32),
            pltpu.VMEM((columns, depth), jnp.bfloat16),
            pltpu.VMEM((columns, depth), jnp.bfloat16),
        ],
        input_output_aliases=aliases,
        cost_estimate=pl.CostEstimate(
            flops=2 * rows * depth * count * LAGS,
            bytes_accessed=2 * rows * count * LAGS,
            transcendentals=0,
        ),
        compiler_params=pltpu.CompilerParams(vmem_limit_bytes=64 << 20),
        name="correlate",
    )(*operands)


def body(raw_samples, channel_of_row, live_channels, band_reach, bin_taper):
    src_count = lax.axis_size("src")
    rcv_count = lax.axis_size("rcv")
    length = raw_samples.shape[2]
    first, second, near = spread(
        raw_samples, channel_of_row, live_channels, bin_taper, src_count, rcv_count
    )
    route = []
    for s in range(src_count):
        for to in range(1, rcv_count):
            if s >= to:
                route.append((s * rcv_count + to, (s - to) * rcv_count + to))
    far = lax.ppermute(second, ("src", "rcv"), route)
    earlier = correlate([first, second], near, band_reach, length)
    return correlate([second], far, band_reach, length, earlier)[0]


def solution(mesh):
    return jax.shard_map(
        body,
        mesh=mesh,
        in_specs=(P("rcv", "src", None), P("src"), P("src"), P("src"), P()),
        out_specs=P("src", "rcv"),
        check_vma=False,
    )
```

time: 100 us -> 88.2 us (0.88)
  the two profiles are of different devices: /device:TPU:19 before, /device:TPU:7 now
where the time goes in v3:
time: 88.2 us; the launch traced here: 88 us
  Pallas kernels  81.6 us (93%)
  waiting for transfers between devices  4.68 us (5%)
  starting transfers between devices  1.47 us (2%)
    pallas_call x2, Pallas kernels, correlate(): pl.pallas_call(functools.partial(correlate_kernel, pieces, half_index, 1....  47 us
    pallas_call x1, Pallas kernels, spread(): pl.pallas_call(functools.partial(spread_kernel, src_count, rcv_count), ou...  34.6 us
    ppermute x1, waiting for transfers between devices, body(): far = lax.ppermute(second, ('src', 'rcv'), route)  4.68 us
  transfers between devices with their start and end apart: 1, of which 1 were waited for; matrix products, arithmetic and copies ran while one was open for 0% of the time, Pallas kernels for 26%

profile of v3, /device:TPU:7, one launch (start us, length us, event | category | flops | bytes accessed | tf_op | source)
XLA Modules:
  0.0 88.0 jit_solution(2317923609969168516)
XLA Ops:
  0.0 34.6 %spread.1 = (bf16[4,3,8,32,128]{4,3,2,1,0:T(8,128)(2,1)}, bf16[4,3,8,32,128]{4,3,2,1,0:T(8,128)(2,1)}, bf16[4,3,8,32,128]{4,3,2,1,0:T(8,128)(2,1)}) custom-call(bf16[3,512,1024]{2,1,0:T(8,128)(2,1)} %raw_ref.1, s32[1,512]{1,0:T(1,128)} %bitcast.4, f32[1,64]{1,0:T(1,128)} %bitcast.6, bf16[1024,128]{1,0:T(8,128)(2,1)} %constant.6.clone.basis_hbm, s32[1,512]{1,0:T(1,128)} %bitcast.5), custom_call_target="tpu_custom_call" | custom-call | tf_op jit(solution)/shard_map/spread/pallas_call | solution.py:302
  34.6 1.5 %collective-permute-start = (bf16[4,3,8,32,128]{4,3,2,1,0:T(8,128)(2,1)}, bf16[4,3,8,32,128]{4,3,2,1,0:T(8,128)(2,1)}, u32[]{:S(2)}, u32[]{:S(2)}) collective-permute-start(bf16[4,3,8,32,128]{4,3,2,1,0:T(8,128)(2,1)} %get-tuple-element.10.refs_1_.refs_0_), channel_id=1, source_target_pairs={{5,1},{9,5},{10,2},{13,9},{14,6},{15,3},{17,13},{18,10},{19,7},{21... | collective-permute-start | bytes 2359304 | tf_op jit(solution)/shard_map/ppermute | solution.py:505
  36.1 22.9 %correlate.2 = (bf16[512,16384]{1,0:T(8,128)(2,1)}, bf16[512,1536]{1,0:T(8,128)(2,1)}) custom-call(bf16[4,3,8,32,128]{4,3,2,1,0:T(8,128)(2,1)} %get-tuple-element.11.refs_0_, bf16[4,3,8,32,128]{4,3,2,1,0:T(8,128)(2,1)} %get-tuple-element.10.refs_1_.refs_0_, bf16[4,3,8,32,128]{4,3,2,1,0:T(8,128)(2,1)} %get-tuple-element.12.refs_2_, s32[1,512]{1,0:T(1,128)} %bitcast.7, ...), custom_call_target="tpu_custom_call" | custom-call | flops 12884901888 | bytes 8388608 | tf_op jit(solution)/shard_map/correlate/pallas_call | solution.py:465
  59.0 4.7 %collective-permute-done.refs_1_ = bf16[4,3,8,32,128]{4,3,2,1,0:T(8,128)(2,1)} collective-permute-done((bf16[4,3,8,32,128]{4,3,2,1,0:T(8,128)(2,1)}, bf16[4,3,8,32,128]{4,3,2,1,0:T(8,128)(2,1)}, u32[]{:S(2)}, u32[]{:S(2)}) %collective-permute-start) | collective-permute-done | bytes 786464 | tf_op jit(solution)/shard_map/ppermute | solution.py:505
  63.7 24.1 %correlate.3 = bf16[512,16384]{1,0:T(8,128)(2,1)} custom-call(bf16[4,3,8,32,128]{4,3,2,1,0:T(8,128)(2,1)} %get-tuple-element.10.refs_1_.refs_0_, bf16[4,3,8,32,128]{4,3,2,1,0:T(8,128)(2,1)} %collective-permute-done.refs_1_, s32[1,512]{1,0:T(1,128)} %bitcast.8, f32[32,128]{1,0:T(8,128)} %constant.7.clone.refs_4_.refs_3_, ...), custom_call_target="tpu_custom_call", output_to_operand_aliasing={{}: (6, {})} | custom-call | flops 12884901888 | bytes 8388608 | tf_op jit(solution)/shard_map/correlate/pallas_call | solution.py:465
Async XLA Ops:
  34.6 29.1 %collective-permute-start = (bf16[4,3,8,32,128]{4,3,2,1,0:T(8,128)(2,1)}, bf16[4,3,8,32,128]{4,3,2,1,0:T(8,128)(2,1)}, u32[]{:S(2)}, u32[]{:S(2)}) collective-permute-start(bf16[4,3,8,32,128]{4,3,2,1,0:T(8,128)(2,1)} %get-tuple-element.10.refs_1_.refs_0_), channel_id=1, source_target_pairs={{5,1},{9,5},{10,2},{13,9},{14,6},{15,3},{17,13},{18,10},{19,7},{21... | collective-permute-start | bytes 2359304 | tf_op jit(solution)/shard_map/ppermute | solution.py:505

commit v4 on v3

--- a/solution.py
+++ b/solution.py
@@ -93,7 +93,7 @@
     src_count, rcv_count, raw_ref, channel_hbm, taper_hbm, basis_hbm, live_hbm,
     first_ref, second_ref, near_ref,
     x_ref, channel_ref, taper_ref, basis_ref, live_ref, mask_ref, normed_ref, ordered_ref, arrived_ref, own_ref,
-    swap_send, swap_recv, block_send, block_recv, pass_send, near_send, near_recv, local_sem,
+    swap_send, swap_recv, block_send, block_recv, pass_send, near_send, near_recv, relay_send, local_sem,
     load_sem, table_sem,
 ):
     src, rcv = lax.axis_index("src"), lax.axis_index("rcv")
@@ -124,9 +124,6 @@
     row, core = rcv // 2, rcv % 2
     mate = rcv + 1 - 2 * core
 
-    def slot(receiver, holder):
-        return (receiver + rcv_count - holder) % rcv_count
-
     def signal(place):
         pl.semaphore_signal(barrier, inc=1, device_id=place, device_id_type=pl.DeviceIdType.MESH)
 
@@ -147,10 +144,18 @@
         signal((src, (rcv + k) % rcv_count))
     takes = (rcv >= 1) & (src + rcv < src_count)
 
-    @pl.when(takes)
+    relayed = (rcv >= 3) & (core == 1)
+    relays = takes & (rcv >= 2) & (core == 0) & (src >= 1)
+    direct = [to for to in range(1, rcv_count) if to == 1 or to % 2 == 0]
+
+    @pl.when(takes & jnp.logical_not(relayed))
     def _():
         for k in range(rcv_count):
             signal((src + rcv, k))
+
+    @pl.when(takes & relayed)
+    def _():
+        signal((src + 1, rcv - 1))
 
     def swap(w, k):
         target = (src + k) % src_count
@@ -174,49 +179,54 @@
 
     def share(w, h, k):
         to = mate if k == 0 else ((row + k) % pairs) * 2 + core
-        place = slot(to, rcv)
         return push(
             own_ref.at[2 * w + h],
-            block_refs[h].at[place, w],
+            block_refs[h].at[rcv, w],
             block_send.at[2 * w + h, k],
-            block_recv.at[2 * w + h, place],
+            block_recv.at[2 * w + h, rcv],
             (src, to),
         )
 
     def shared(w, h, holder):
-        place = slot(rcv, holder)
         return push(
             own_ref.at[2 * w + h],
-            block_refs[h].at[place, w],
+            block_refs[h].at[holder, w],
             block_send.at[2 * w + h, 0],
-            block_recv.at[2 * w + h, place],
+            block_recv.at[2 * w + h, holder],
             (src, mate),
         )
 
     def hand_on(w, h, k):
         holder = ((row + k) % pairs) * 2 + core
-        place = slot(mate, holder)
-        return push(
-            block_refs[h].at[slot(rcv, holder), w],
-            block_refs[h].at[place, w],
+        return push(
+            block_refs[h].at[holder, w],
+            block_refs[h].at[holder, w],
             pass_send.at[2 * w + h, k],
-            block_recv.at[2 * w + h, place],
+            block_recv.at[2 * w + h, holder],
             (src, mate),
         )
 
     def near(w, to):
-        place = slot(to, rcv)
         return push(
             own_ref.at[2 * w],
-            near_ref.at[place, w],
+            near_ref.at[rcv, w],
             near_send.at[w, to],
-            near_recv.at[w, place],
+            near_recv.at[w, rcv],
             (src - to, to),
+        )
+
+    def relay(w, k):
+        return push(
+            near_ref.at[k, w],
+            near_ref.at[k, w],
+            relay_send.at[w, k],
+            near_recv.at[w, k],
+            (src - 1, rcv + 1),
         )
 
     def keep(w, h):
         return pltpu.make_async_copy(
-            own_ref.at[2 * w + h], block_refs[h].at[0, w], local_sem.at[2 * w + h]
+            own_ref.at[2 * w + h], block_refs[h].at[rcv, w], local_sem.at[2 * w + h]
         )
 
     for table in tables:
@@ -235,9 +245,10 @@
             w, src_count, x_ref, channel_ref, taper_ref, basis_ref, normed_ref
         )
         if w == 0:
-            pl.semaphore_wait(
-                barrier, src_count - 1 + rcv_count - 1 + jnp.minimum(src, rcv_count - 1)
-            )
+            expected = src_count - 1 + rcv_count - 1 + jnp.where(relays, 1, 0)
+            for to in direct:
+                expected = expected + jnp.where(src >= to, 1, 0)
+            pl.semaphore_wait(barrier, expected)
         for k in range(1, src_count):
             swap(w, k).start()
 
@@ -256,7 +267,7 @@
             for k in range(pairs):
                 share(w, h, (k + 1) % pairs).start()
             if h == 0:
-                for to in range(1, rcv_count):
+                for to in direct:
                     pl.when(src >= to)(lambda w=w, to=to: near(w, to).start())
             keep(w, h).start()
 
@@ -267,16 +278,17 @@
                 hand_on(w, h, k).start()
 
     for w in range(windows):
+        for k in range(rcv_count):
+            arrival = push(
+                near_ref.at[k, w], near_ref.at[k, w], near_send.at[w, 0], near_recv.at[w, k], (src, mate)
+            )
+            pl.when(takes)(lambda arrival=arrival: arrival.wait_recv())
+            pl.when(relays)(lambda w=w, k=k: relay(w, k).start())
+
+    for w in range(windows):
         for h in range(2):
             for k in range(pairs):
                 shared(w, h, ((row + k) % pairs) * 2 + 1 - core).wait_recv()
-
-        @pl.when(takes)
-        def _(w=w):
-            for k in range(rcv_count):
-                push(
-                    own_ref.at[2 * w], near_ref.at[k, w], near_send.at[w, 0], near_recv.at[w, k], (src + rcv, k)
-                ).wait_recv()
 
         for k in range(1, src_count):
             swap(w, k).wait_send()
@@ -286,8 +298,13 @@
                 if k:
                     hand_on(w, h, k).wait_send()
             keep(w, h).wait()
-        for to in range(1, rcv_count):
+        for to in direct:
             pl.when(src >= to)(lambda w=w, to=to: near(w, to).wait_send())
+
+        @pl.when(relays)
+        def _(w=w):
+            for k in range(rcv_count):
+                relay(w, k).wait_send()
 
 
 def spread(raw_samples, channel_of_row, live_channels, bin_taper, src_count, rcv_count):
@@ -320,6 +337,7 @@
             dma((2 * windows, rcv_count // 2)),
             dma((2 * windows, rcv_count)),
             dma((2 * windows, rcv_count // 2)),
+            dma((windows, rcv_count)),
             dma((windows, rcv_count)),
             dma((windows, rcv_count)),
             dma((2 * windows,)),
@@ -501,7 +519,8 @@
     for s in range(src_count):
         for to in range(1, rcv_count):
             if s >= to:
-                route.append((s * rcv_count + to, (s - to) * rcv_count + to))
+                holder = to if to < 3 or to % 2 == 0 else (to - 2 if to > 3 else 0)
+                route.append((s * rcv_count + holder, (s - to) * rcv_count + to))
     far = lax.ppermute(second, ("src", "rcv"), route)
     earlier = correlate([first, second], near, band_reach, length)
     return correlate([second], far, band_reach, length, earlier)[0]

time: 88.2 us -> 89.4 us (1.014)
  the two profiles are of different devices: /device:TPU:7 before, /device:TPU:16 now
where the time goes in v4:
time: 89.4 us; the launch traced here: 89.2 us
  Pallas kernels  74.3 us (83%)
  starting transfers between devices  14.6 us (16%)
    pallas_call x2, Pallas kernels, correlate(): pl.pallas_call(functools.partial(correlate_kernel, pieces, half_index, 1....  47.1 us
    pallas_call x1, Pallas kernels, spread(): pl.pallas_call(functools.partial(spread_kernel, src_count, rcv_count), ou...  27.2 us
    ppermute x1, starting transfers between devices, body(): far = lax.ppermute(second, ('src', 'rcv'), route)  14.6 us
  transfers between devices with their start and end apart: 1, of which 0 were waited for; matrix products, arithmetic and copies ran while one was open for 0% of the time, Pallas kernels for 26%

profile of v4, /device:TPU:16, one launch (start us, length us, event | category | flops | bytes accessed | tf_op | source)
XLA Modules:
  0.0 89.2 jit_solution(2786634866315441721)
XLA Ops:
  0.0 27.2 %spread.1 = (bf16[4,3,8,32,128]{4,3,2,1,0:T(8,128)(2,1)}, bf16[4,3,8,32,128]{4,3,2,1,0:T(8,128)(2,1)}, bf16[4,3,8,32,128]{4,3,2,1,0:T(8,128)(2,1)}) custom-call(bf16[3,512,1024]{2,1,0:T(8,128)(2,1)} %raw_ref.1, s32[1,512]{1,0:T(1,128)} %bitcast.4, f32[1,64]{1,0:T(1,128)} %bitcast.6, bf16[1024,128]{1,0:T(8,128)(2,1)} %constant.6.clone.basis_hbm, s32[1,512]{1,0:T(1,128)} %bitcast.5), custom_call_target="tpu_custom_call" | custom-call | tf_op jit(solution)/shard_map/spread/pallas_call | solution.py:319
  27.2 14.6 %collective-permute-start = (bf16[4,3,8,32,128]{4,3,2,1,0:T(8,128)(2,1)}, bf16[4,3,8,32,128]{4,3,2,1,0:T(8,128)(2,1)}, u32[]{:S(2)}, u32[]{:S(2)}) collective-permute-start(bf16[4,3,8,32,128]{4,3,2,1,0:T(8,128)(2,1)} %get-tuple-element.10.refs_1_.refs_0_), channel_id=1, source_target_pairs={{5,1},{9,5},{10,2},{13,9},{14,6},{12,3},{17,13},{18,10},{16,7},{21... | collective-permute-start | bytes 2359304 | tf_op jit(solution)/shard_map/ppermute | solution.py:524
  41.9 22.9 %correlate.2 = (bf16[512,16384]{1,0:T(8,128)(2,1)}, bf16[512,1536]{1,0:T(8,128)(2,1)}) custom-call(bf16[4,3,8,32,128]{4,3,2,1,0:T(8,128)(2,1)} %get-tuple-element.11.refs_0_, bf16[4,3,8,32,128]{4,3,2,1,0:T(8,128)(2,1)} %get-tuple-element.10.refs_1_.refs_0_, bf16[4,3,8,32,128]{4,3,2,1,0:T(8,128)(2,1)} %get-tuple-element.12.refs_2_, s32[1,512]{1,0:T(1,128)} %bitcast.7, ...), custom_call_target="tpu_custom_call" | custom-call | flops 12884901888 | bytes 8388608 | tf_op jit(solution)/shard_map/correlate/pallas_call | solution.py:483
  64.8 0.0 collective-permute-done.refs_1_
  64.8 24.2 %correlate.3 = bf16[512,16384]{1,0:T(8,128)(2,1)} custom-call(bf16[4,3,8,32,128]{4,3,2,1,0:T(8,128)(2,1)} %get-tuple-element.10.refs_1_.refs_0_, bf16[4,3,8,32,128]{4,3,2,1,0:T(8,128)(2,1)} %collective-permute-done.refs_1_, s32[1,512]{1,0:T(1,128)} %bitcast.8, f32[32,128]{1,0:T(8,128)} %constant.7.clone.refs_4_.refs_3_, ...), custom_call_target="tpu_custom_call", output_to_operand_aliasing={{}: (6, {})} | custom-call | flops 12884901888 | bytes 8388608 | tf_op jit(solution)/shard_map/correlate/pallas_call | solution.py:483
Async XLA Ops:
  27.2 37.6 %collective-permute-start = (bf16[4,3,8,32,128]{4,3,2,1,0:T(8,128)(2,1)}, bf16[4,3,8,32,128]{4,3,2,1,0:T(8,128)(2,1)}, u32[]{:S(2)}, u32[]{:S(2)}) collective-permute-start(bf16[4,3,8,32,128]{4,3,2,1,0:T(8,128)(2,1)} %get-tuple-element.10.refs_1_.refs_0_), channel_id=1, source_target_pairs={{5,1},{9,5},{10,2},{13,9},{14,6},{12,3},{17,13},{18,10},{16,7},{21... | collective-permute-start | bytes 2359304 | tf_op jit(solution)/shard_map/ppermute | solution.py:524

commit v5 on v4

--- a/solution.py
+++ b/solution.py
@@ -15,6 +15,7 @@
 HW = 64
 LAGS = 32
 CHUNK = 16
+GROUP = 16
 
 norm_floor = 1e-05
 water_level = 0.3
@@ -37,8 +38,8 @@
     scale = 1.0 / math.sqrt(F)
     cosine = (np.cos(angle) * scale).astype(np.float32).astype(ml_dtypes.bfloat16)
     sine = (np.sin(angle) * scale).astype(np.float32).astype(ml_dtypes.bfloat16)
-    straight = np.concatenate([cosine, cosine], axis=1).astype(np.float32)
-    swapped = np.concatenate([-sine, sine], axis=1).astype(np.float32)
+    straight = np.concatenate([cosine, cosine], axis=1)
+    swapped = np.concatenate([-sine, sine], axis=1)
     return straight, swapped
 
 
@@ -93,7 +94,7 @@
     src_count, rcv_count, raw_ref, channel_hbm, taper_hbm, basis_hbm, live_hbm,
     first_ref, second_ref, near_ref,
     x_ref, channel_ref, taper_ref, basis_ref, live_ref, mask_ref, normed_ref, ordered_ref, arrived_ref, own_ref,
-    swap_send, swap_recv, block_send, block_recv, pass_send, near_send, near_recv, relay_send, local_sem,
+    swap_send, swap_recv, block_send, block_recv, pass_send, near_send, near_recv, local_sem,
     load_sem, table_sem,
 ):
     src, rcv = lax.axis_index("src"), lax.axis_index("rcv")
@@ -144,18 +145,12 @@
         signal((src, (rcv + k) % rcv_count))
     takes = (rcv >= 1) & (src + rcv < src_count)
 
-    relayed = (rcv >= 3) & (core == 1)
-    relays = takes & (rcv >= 2) & (core == 0) & (src >= 1)
-    direct = [to for to in range(1, rcv_count) if to == 1 or to % 2 == 0]
-
-    @pl.when(takes & jnp.logical_not(relayed))
+    direct = list(range(rcv_count - 1, 0, -1))
+
+    @pl.when(takes)
     def _():
         for k in range(rcv_count):
             signal((src + rcv, k))
-
-    @pl.when(takes & relayed)
-    def _():
-        signal((src + 1, rcv - 1))
 
     def swap(w, k):
         target = (src + k) % src_count
@@ -213,15 +208,6 @@
             near_send.at[w, to],
             near_recv.at[w, rcv],
             (src - to, to),
-        )
-
-    def relay(w, k):
-        return push(
-            near_ref.at[k, w],
-            near_ref.at[k, w],
-            relay_send.at[w, k],
-            near_recv.at[w, k],
-            (src - 1, rcv + 1),
         )
 
     def keep(w, h):
@@ -245,7 +231,7 @@
             w, src_count, x_ref, channel_ref, taper_ref, basis_ref, normed_ref
         )
         if w == 0:
-            expected = src_count - 1 + rcv_count - 1 + jnp.where(relays, 1, 0)
+            expected = src_count - 1 + rcv_count - 1
             for to in direct:
                 expected = expected + jnp.where(src >= to, 1, 0)
             pl.semaphore_wait(barrier, expected)
@@ -283,7 +269,6 @@
                 near_ref.at[k, w], near_ref.at[k, w], near_send.at[w, 0], near_recv.at[w, k], (src, mate)
             )
             pl.when(takes)(lambda arrival=arrival: arrival.wait_recv())
-            pl.when(relays)(lambda w=w, k=k: relay(w, k).start())
 
     for w in range(windows):
         for h in range(2):
@@ -300,11 +285,6 @@
             keep(w, h).wait()
         for to in direct:
             pl.when(src >= to)(lambda w=w, to=to: near(w, to).wait_send())
-
-        @pl.when(relays)
-        def _(w=w):
-            for k in range(rcv_count):
-                relay(w, k).wait_send()
 
 
 def spread(raw_samples, channel_of_row, live_channels, bin_taper, src_count, rcv_count):
@@ -339,7 +319,6 @@
             dma((2 * windows, rcv_count // 2)),
             dma((windows, rcv_count)),
             dma((windows, rcv_count)),
-            dma((windows, rcv_count)),
             dma((2 * windows,)),
             dma((windows,)),
             dma((4,)),
@@ -376,15 +355,17 @@
     src, rcv = lax.axis_index("src"), lax.axis_index("rcv")
 
     def rotate(first, target):
-        straight = straight_ref[...][None]
-        swapped = swapped_ref[...][None]
         for w in range(windows):
-            plain = rcv_ref[pl.ds(first, CHUNK), w * lanes : (w + 1) * lanes]
-            turned = turned_ref[pl.ds(first, CHUNK), w * lanes : (w + 1) * lanes]
-            value = plain[:, None, :] * straight + turned[:, None, :] * swapped
-            target[:, w * lanes : (w + 1) * lanes] = value.reshape(columns, lanes).astype(
-                jnp.bfloat16
-            )
+            span = slice(w * lanes, (w + 1) * lanes)
+            shape = (CHUNK, GROUP, lanes)
+            plain = rcv_ref[pl.ds(first, CHUNK), span]
+            turned = turned_ref[pl.ds(first, CHUNK), span]
+            plain = jnp.broadcast_to(plain[:, None, :], shape).astype(jnp.bfloat16)
+            turned = jnp.broadcast_to(turned[:, None, :], shape).astype(jnp.bfloat16)
+            for lag in range(0, LAGS, GROUP):
+                straight = straight_ref[lag : lag + GROUP][None]
+                swapped = swapped_ref[lag : lag + GROUP][None]
+                target[:, lag : lag + GROUP, span] = plain * straight + turned * swapped
 
     @pl.when(step == 0)
     def _():
@@ -438,7 +419,10 @@
 
     def multiply(source, turn):
         total = lax.dot_general(
-            left_ref[...], source[...], (((1,), (1,)), ((), ())), preferred_element_type=jnp.float32
+            left_ref[...],
+            source[...].reshape(columns, windows * lanes),
+            (((1,), (1,)), ((), ())),
+            preferred_element_type=jnp.float32,
         )
         column = lax.broadcasted_iota(jnp.int32, (1, columns), 1)
         column = column + (2 * step + turn) * columns + half_index * count * LAGS
@@ -488,14 +472,14 @@
         out_specs=out_specs,
         scratch_shapes=[
             pltpu.VMEM((1, rows), jnp.int32),
-            pltpu.VMEM((LAGS, lanes), jnp.float32),
-            pltpu.VMEM((LAGS, lanes), jnp.float32),
+            pltpu.VMEM((LAGS, lanes), jnp.bfloat16),
+            pltpu.VMEM((LAGS, lanes), jnp.bfloat16),
             pltpu.SemaphoreType.DMA((3,)),
             pltpu.VMEM((rows, 1), jnp.int32),
             pltpu.VMEM((count, depth), jnp.float32),
             pltpu.VMEM((count, depth), jnp.float32),
-            pltpu.VMEM((columns, depth), jnp.bfloat16),
-            pltpu.VMEM((columns, depth), jnp.bfloat16),
+            pltpu.VMEM((CHUNK, LAGS, depth), jnp.bfloat16),
+            pltpu.VMEM((CHUNK, LAGS, depth), jnp.bfloat16),
         ],
         input_output_aliases=aliases,
         cost_estimate=pl.CostEstimate(

time: 89.4 us -> 88.4 us (0.989)
  the two profiles are of different devices: /device:TPU:16 before, /device:TPU:7 now
where the time goes in v5:
time: 88.4 us; the launch traced here: 88.2 us
  Pallas kernels  77.6 us (88%)
  waiting for transfers between devices  8.95 us (10%)
  starting transfers between devices  1.47 us (2%)
    pallas_call x2, Pallas kernels, correlate(): pl.pallas_call(functools.partial(correlate_kernel, pieces, half_index, 1....  45.4 us
    pallas_call x1, Pallas kernels, spread(): pl.pallas_call(functools.partial(spread_kernel, src_count, rcv_count), ou...  32.2 us
    ppermute x1, waiting for transfers between devices, body(): far = lax.ppermute(second, ('src', 'rcv'), route)  8.95 us
  transfers between devices with their start and end apart: 1, of which 1 were waited for; matrix products, arithmetic and copies ran while one was open for 0% of the time, Pallas kernels for 25%

profile of v5, /device:TPU:7, one launch (start us, length us, event | category | flops | bytes accessed | tf_op | source)
XLA Modules:
  0.0 88.2 jit_solution(11356302140193195051)
XLA Ops:
  0.0 32.2 %spread.1 = (bf16[4,3,8,32,128]{4,3,2,1,0:T(8,128)(2,1)}, bf16[4,3,8,32,128]{4,3,2,1,0:T(8,128)(2,1)}, bf16[4,3,8,32,128]{4,3,2,1,0:T(8,128)(2,1)}) custom-call(bf16[3,512,1024]{2,1,0:T(8,128)(2,1)} %raw_ref.1, s32[1,512]{1,0:T(1,128)} %bitcast.4, f32[1,64]{1,0:T(1,128)} %bitcast.6, bf16[1024,128]{1,0:T(8,128)(2,1)} %constant.6.clone.basis_hbm, s32[1,512]{1,0:T(1,128)} %bitcast.5), custom_call_target="tpu_custom_call" | custom-call | tf_op jit(solution)/shard_map/spread/pallas_call | solution.py:299
  32.2 1.5 %collective-permute-start = (bf16[4,3,8,32,128]{4,3,2,1,0:T(8,128)(2,1)}, bf16[4,3,8,32,128]{4,3,2,1,0:T(8,128)(2,1)}, u32[]{:S(2)}, u32[]{:S(2)}) collective-permute-start(bf16[4,3,8,32,128]{4,3,2,1,0:T(8,128)(2,1)} %get-tuple-element.10.refs_1_.refs_0_), channel_id=1, source_target_pairs={{5,1},{9,5},{10,2},{13,9},{14,6},{12,3},{17,13},{18,10},{16,7},{21... | collective-permute-start | bytes 2359304 | tf_op jit(solution)/shard_map/ppermute | solution.py:508
  33.7 22.1 %correlate.2 = (bf16[512,16384]{1,0:T(8,128)(2,1)}, bf16[512,1536]{1,0:T(8,128)(2,1)}) custom-call(bf16[4,3,8,32,128]{4,3,2,1,0:T(8,128)(2,1)} %get-tuple-element.11.refs_0_, bf16[4,3,8,32,128]{4,3,2,1,0:T(8,128)(2,1)} %get-tuple-element.10.refs_1_.refs_0_, bf16[4,3,8,32,128]{4,3,2,1,0:T(8,128)(2,1)} %get-tuple-element.12.refs_2_, s32[1,512]{1,0:T(1,128)} %bitcast.7, ...), custom_call_target="tpu_custom_call" | custom-call | flops 12884901888 | bytes 8388608 | tf_op jit(solution)/shard_map/correlate/pallas_call | solution.py:467
  55.9 8.9 %collective-permute-done.refs_1_ = bf16[4,3,8,32,128]{4,3,2,1,0:T(8,128)(2,1)} collective-permute-done((bf16[4,3,8,32,128]{4,3,2,1,0:T(8,128)(2,1)}, bf16[4,3,8,32,128]{4,3,2,1,0:T(8,128)(2,1)}, u32[]{:S(2)}, u32[]{:S(2)}) %collective-permute-start) | collective-permute-done | bytes 786464 | tf_op jit(solution)/shard_map/ppermute | solution.py:508
  64.8 23.2 %correlate.3 = bf16[512,16384]{1,0:T(8,128)(2,1)} custom-call(bf16[4,3,8,32,128]{4,3,2,1,0:T(8,128)(2,1)} %get-tuple-element.10.refs_1_.refs_0_, bf16[4,3,8,32,128]{4,3,2,1,0:T(8,128)(2,1)} %collective-permute-done.refs_1_, s32[1,512]{1,0:T(1,128)} %bitcast.8, bf16[32,128]{1,0:T(8,128)(2,1)} %constant.7.clone.refs_4_.refs_3_, ...), custom_call_target="tpu_custom_call", output_to_operand_aliasing={{}: (6, {})} | custom-call | flops 12884901888 | bytes 8388608 | tf_op jit(solution)/shard_map/correlate/pallas_call | solution.py:467
Async XLA Ops:
  32.2 32.6 %collective-permute-start = (bf16[4,3,8,32,128]{4,3,2,1,0:T(8,128)(2,1)}, bf16[4,3,8,32,128]{4,3,2,1,0:T(8,128)(2,1)}, u32[]{:S(2)}, u32[]{:S(2)}) collective-permute-start(bf16[4,3,8,32,128]{4,3,2,1,0:T(8,128)(2,1)} %get-tuple-element.10.refs_1_.refs_0_), channel_id=1, source_target_pairs={{5,1},{9,5},{10,2},{13,9},{14,6},{12,3},{17,13},{18,10},{16,7},{21... | collective-permute-start | bytes 2359304 | tf_op jit(solution)/shard_map/ppermute | solution.py:508
